TPU v7x, 32 devices: a whole 2x2x4 slice. The times are simulated.
32 devices in a mesh: head: 4 (over x, core), blk: 8 (over z, y).
Axes of the slice: x: 2, y: 2, z: 4, core: 2. Of those that a mesh axis runs over, the one named last changes fastest.
Arguments:
- tokens_in: bfloat16 [8, 4096, 768], P('blk', 'head'), may hold values from -6 to 6
- query_weight: float32 [768, 768], P(('head', 'blk')), may hold values from -0.21875 to 0.21875
- query_bias: float32 [768], P(('head', 'blk')), may hold values from -3 to 3
- key_weight: float32 [768, 768], P(('head', 'blk')), may hold values from -0.21875 to 0.21875
- value_weight: float32 [768, 768], P(('head', 'blk')), may hold values from -0.21875 to 0.21875
- value_bias: float32 [768], P(('head', 'blk')), may hold values from -3 to 3
- mixer_weight: float32 [768, 768], P(('head', 'blk')), may hold values from -3.5 to 3.5
- mixer_bias: float32 [768], P(('head', 'blk')), may hold values from -2 to 2
- first_gain: float32 [768], P(('head', 'blk')), may hold values from 0.5 to 1.5
- first_shift: float32 [768], P(('head', 'blk')), may hold values from -2 to 2
- expand_weight: float32 [768, 3072], P(('head', 'blk')), may hold values from -0.21875 to 0.21875
- expand_bias: float32 [3072], P(('head', 'blk')), may hold values from -3 to 3
- shrink_weight: float32 [3072, 768], P(('head', 'blk')), may hold values from -0.109375 to 0.109375
- shrink_bias: float32 [768], P(('head', 'blk')), may hold values from -2 to 2
- second_gain: float32 [768], P(('head', 'blk')), may hold values from 0.5 to 1.5
- second_shift: float32 [768], P(('head', 'blk')), may hold values from -2 to 2
- doc_starts: int32 [12], replicated, may hold values from 0 to 32767, as said below
- random_blocks: int32 [512, 3], P('blk'), may hold values from 0 to 511, as said below
- cotangent: bfloat16 [8, 4096, 768], P('blk', 'head'), may hold values from -6 to 6
Outputs:
- layer_out: bfloat16 [8, 4096, 768], P('blk', 'head')
- input_grad: float32 [8, 4096, 768], P('blk', 'head')
- query_weight_grad: float32 [768, 768], P(('head', 'blk'))
- query_bias_grad: float32 [768], P(('head', 'blk'))
- key_weight_grad: float32 [768, 768], P(('head', 'blk'))
- value_weight_grad: float32 [768, 768], P(('head', 'blk'))
- value_bias_grad: float32 [768], P(('head', 'blk'))
- mixer_weight_grad: float32 [768, 768], P(('head', 'blk'))
- mixer_bias_grad: float32 [768], P(('head', 'blk'))
- first_gain_grad: float32 [768], P(('head', 'blk'))
- first_shift_grad: float32 [768], P(('head', 'blk'))
- expand_weight_grad: float32 [768, 3072], P(('head', 'blk'))
- expand_bias_grad: float32 [3072], P(('head', 'blk'))
- shrink_weight_grad: float32 [3072, 768], P(('head', 'blk'))
- shrink_bias_grad: float32 [768], P(('head', 'blk'))
- second_gain_grad: float32 [768], P(('head', 'blk'))
- second_shift_grad: float32 [768], P(('head', 'blk'))
Inputs may be any that keep to these rules, and one draw needn't show every extreme that they name: Increasing, doc_starts[0] = 0; a document runs from its start to the next start, the last one to 32768; every document holds between 1365 and 4096 tokens, and one holds exactly 4096. `random_blocks`: each entry of row j is a block holding some token of the document of position 64 * j; entries may repeat.
All inputs are finite; a program needn't handle non-finite values.
Results may differ from a plain program's by a relative error of at most 0.014.
The roundings to bfloat16 on the way count: a program that leaves them out, or rounds other values in their place, can miss the bound.
Values may be sent and summed in bfloat16 or wider, within the bound.
No kernel may reach another device: no remote copies, remote signals or barrier semaphores. Data moves between devices by JAX's collectives and lax.ppermute only.
A program may use at most 256 MiB of HBM per device.

v0:
```python
import math

import jax
import jax.numpy as jnp
from jax import lax
from jax.sharding import PartitionSpec as P

HEADS = 12
HEAD_DIM = 64
BLOCK = 64
GLOBAL_BLOCKS = 2
MAXDOC = 4096


layer_eps = 1e-12
masked_score = -1e30


def shifted(array, axis, by):
    count = lax.axis_size(axis)
    pairs = [(i, i + by) for i in range(count) if 0 <= i + by < count]
    return lax.ppermute(array, axis, pairs)


def token_docs(positions, starts):
    before = starts[None, :] <= positions[:, None]
    doc_index = jnp.sum(before.astype(jnp.int32), axis=1) - 1
    doc_first = jnp.max(jnp.where(before, starts[None, :], 0), axis=1)
    return (doc_index, doc_first)


def block_lists(block_ids, random_picks, starts, total_blocks):
    lead_tokens = block_ids * BLOCK
    first_lead = token_docs(lead_tokens, starts)[1]
    first_tail = token_docs(lead_tokens + BLOCK - 1, starts)[1]
    columns = [block_ids - 1, block_ids, block_ids + 1]
    columns += [random_picks[:, pick] for pick in range(random_picks.shape[1])]
    for anchor in (first_lead, first_tail):
        columns += [anchor // BLOCK + offset for offset in range(GLOBAL_BLOCKS + 1)]
    candidate = jnp.clip(jnp.stack(columns, axis=1), 0, total_blocks - 1)
    repeats = [jnp.zeros(candidate.shape[:1], dtype=jnp.bool_)]
    for column in range(1, candidate.shape[1]):
        repeats.append(jnp.any(candidate[:, :column] == candidate[:, column : column + 1], axis=1))
    distinct = jnp.logical_not(jnp.stack(repeats, axis=1))
    nearby = jnp.logical_or(
        jnp.abs(candidate - block_ids[:, None]) <= 1,
        jnp.any(candidate[:, :, None] == random_picks[:, None, :], axis=2),
    )
    return (candidate, distinct, nearby)


def allowed_mask(key_doc, candidate, distinct, nearby, query_doc, query_first):
    key_pos = candidate[..., None] * BLOCK + jnp.arange(BLOCK, dtype=jnp.int32)
    same_doc = key_doc[:, None] == query_doc[:, :, None, None]
    early_key = key_pos[:, None] - query_first[:, :, None, None] < GLOBAL_BLOCKS * BLOCK
    return same_doc & distinct[:, None, :, None] & (nearby[:, None, :, None] | early_key)


def norm_rows(values_in, gain_row, shift_row):
    row_mean = jnp.mean(values_in, axis=-1, keepdims=True)
    centred = values_in - row_mean
    spread = jnp.mean(centred * centred, axis=-1, keepdims=True)
    return centred * lax.rsqrt(spread + layer_eps) * gain_row + shift_row


def gelu_exact(values_in):
    return jax.nn.gelu(values_in, approximate=False)


def neighbour_keys(pair_rows):
    carried = pair_rows
    carried = shifted(carried, "blk", 1)
    lower = [carried]
    carried = pair_rows
    carried = shifted(carried, "blk", -1)
    upper = [carried]
    return jnp.concatenate(lower[::-1] + [pair_rows] + upper, axis=0)


def body(
    tokens_in,
    query_weight,
    query_bias,
    key_weight,
    value_weight,
    value_bias,
    mixer_weight,
    mixer_bias,
    first_gain,
    first_shift,
    expand_weight,
    expand_bias,
    shrink_weight,
    shrink_bias,
    second_gain,
    second_shift,
    doc_starts,
    random_blocks,
    cotangent,
):
    f32 = jnp.float32
    bf16 = jnp.bfloat16
    head_count = lax.axis_size("head")
    cycle_size = lax.axis_size("blk")
    cycle_index = lax.axis_index("blk")
    local_rows = tokens_in.shape[1]
    model_width = tokens_in.shape[2]
    segment = local_rows * head_count
    local_blocks = segment // BLOCK
    total_blocks = local_blocks * cycle_size
    reach_steps = -(-MAXDOC // segment)
    group_heads = HEADS // head_count
    head_slab = group_heads * HEAD_DIM
    group_blocks = math.gcd(local_blocks, 8)
    group_count = local_blocks // group_blocks
    score_scale = HEAD_DIM ** (-0.5)
    masters = (
        query_weight,
        query_bias,
        key_weight,
        value_weight,
        value_bias,
        mixer_weight,
        mixer_bias,
        first_gain,
        first_shift,
        expand_weight,
        expand_bias,
        shrink_weight,
        shrink_bias,
        second_gain,
        second_shift,
    )
    shards = [master.astype(bf16) for master in masters]
    gathered = (
        lax.all_gather(shards[0], ("head", "blk"), axis=0, tiled=True),
        lax.all_gather(shards[1], ("head", "blk"), axis=0, tiled=True),
        lax.all_gather(shards[2], ("head", "blk"), axis=0, tiled=True),
        lax.all_gather(shards[3], ("head", "blk"), axis=0, tiled=True),
        lax.all_gather(shards[4], ("head", "blk"), axis=0, tiled=True),
        lax.all_gather(shards[5], ("head", "blk"), axis=0, tiled=True),
        lax.all_gather(shards[6], ("head", "blk"), axis=0, tiled=True),
        lax.all_gather(shards[7], ("head", "blk"), axis=0, tiled=True),
        lax.all_gather(shards[8], ("head", "blk"), axis=0, tiled=True),
        lax.all_gather(shards[9], ("head", "blk"), axis=0, tiled=True),
        lax.all_gather(shards[10], ("head", "blk"), axis=0, tiled=True),
        lax.all_gather(shards[11], ("head", "blk"), axis=0, tiled=True),
        lax.all_gather(shards[12], ("head", "blk"), axis=0, tiled=True),
        lax.all_gather(shards[13], ("head", "blk"), axis=0, tiled=True),
        lax.all_gather(shards[14], ("head", "blk"), axis=0, tiled=True),
    )
    (
        query_matrix,
        query_offset,
        key_matrix,
        value_matrix,
        value_offset,
        mixer_matrix,
        mixer_offset,
        first_scale,
        first_level,
        expand_matrix,
        expand_offset,
        shrink_matrix,
        shrink_offset,
        second_scale,
        second_level,
    ) = gathered
    inputs = tokens_in[0]
    input_wide = inputs.astype(f32)
    query_rows = (
        jnp.dot(inputs, query_matrix, preferred_element_type=f32) + query_offset.astype(f32)
    ).astype(bf16)
    key_rows = jnp.dot(inputs, key_matrix, preferred_element_type=f32).astype(bf16)
    value_rows = (
        jnp.dot(inputs, value_matrix, preferred_element_type=f32) + value_offset.astype(f32)
    ).astype(bf16)
    packed = jnp.concatenate(
        [
            query_rows.reshape(local_rows, head_count, head_slab),
            key_rows.reshape(local_rows, head_count, head_slab),
            value_rows.reshape(local_rows, head_count, head_slab),
        ],
        axis=2,
    )
    by_heads = lax.all_to_all(packed, "head", split_axis=1, concat_axis=0, tiled=True).reshape(
        segment, 3 * head_slab
    )
    query_seg = by_heads[:, :head_slab]
    pair_seg = by_heads[:, head_slab:]
    key_pool = neighbour_keys(pair_seg)
    pool_blocks = key_pool.reshape(-1, BLOCK, 2 * head_slab)
    pool_count = pool_blocks.shape[0]
    pool_positions = (cycle_index - reach_steps) * segment + jnp.arange(
        key_pool.shape[0], dtype=jnp.int32
    )
    key_doc_blocks = token_docs(pool_positions, doc_starts)[0].reshape(-1, BLOCK)
    query_positions = cycle_index * segment + jnp.arange(segment, dtype=jnp.int32)
    query_doc, query_first = token_docs(query_positions, doc_starts)
    block_ids = cycle_index * local_blocks + jnp.arange(local_blocks, dtype=jnp.int32)
    candidate, distinct, nearby = block_lists(block_ids, random_blocks, doc_starts, total_blocks)
    local_ids = candidate - (cycle_index - reach_steps) * local_blocks
    inside = (local_ids >= 0) & (local_ids < pool_count)
    distinct = distinct & inside
    local_ids = jnp.clip(local_ids, 0, pool_count - 1)

    def grouped(array):
        return array.reshape((group_count, group_blocks) + array.shape[1:])

    query_groups = grouped(query_seg.reshape(local_blocks, BLOCK, group_heads, HEAD_DIM))
    pieces = (
        query_groups,
        grouped(query_doc.reshape(local_blocks, BLOCK)),
        grouped(query_first.reshape(local_blocks, BLOCK)),
        grouped(candidate),
        grouped(local_ids),
        grouped(distinct),
        grouped(nearby),
    )

    def group_scores(pool_now, group_piece):
        (
            group_query,
            group_doc,
            group_first,
            group_cand,
            group_local,
            group_distinct,
            group_nearby,
        ) = group_piece
        fetched = pool_now[group_local]
        key_part = fetched[..., :head_slab].reshape(fetched.shape[:3] + (group_heads, HEAD_DIM))
        value_part = fetched[..., head_slab:].reshape(group_blocks, -1, group_heads, HEAD_DIM)
        raw_scores = jnp.einsum(
            "gqhd,gckhd->ghqck", group_query, key_part, preferred_element_type=f32
        )
        key_mask = allowed_mask(
            key_doc_blocks[group_local],
            group_cand,
            group_distinct,
            group_nearby,
            group_doc,
            group_first,
        )
        scores = jnp.where(key_mask[:, None], raw_scores * score_scale, masked_score)
        return (scores.reshape(group_blocks, group_heads, BLOCK, -1), key_part, value_part)

    def attend(group_piece):
        scores, key_part, value_part = group_scores(pool_blocks, group_piece)
        row_top = jnp.max(scores, axis=-1, keepdims=True)
        row_exp = jnp.exp(scores - row_top)
        row_total = jnp.sum(row_exp, axis=-1, keepdims=True)
        soft_low = (row_exp / row_total).astype(bf16)
        mixed_out = jnp.einsum(
            "ghqn,gnhd->gqhd", soft_low, value_part, preferred_element_type=f32
        ).astype(bf16)
        return (mixed_out, (row_top + jnp.log(row_total))[..., 0])

    mixed_groups, lse_groups = lax.map(attend, pieces)
    attended = lax.all_to_all(
        mixed_groups.reshape(segment, 1, head_slab), "head", split_axis=0, concat_axis=1, tiled=True
    ).reshape(local_rows, model_width)
    first_sum = (
        input_wide
        + jnp.dot(attended, mixer_matrix, preferred_element_type=f32)
        + mixer_offset.astype(f32)
    )
    middle, first_back = jax.vjp(
        norm_rows, first_sum, first_scale.astype(f32), first_level.astype(f32)
    )
    middle_low = middle.astype(bf16)
    pre_act = jnp.dot(middle_low, expand_matrix, preferred_element_type=f32) + expand_offset.astype(
        f32
    )
    active_wide, gelu_back = jax.vjp(gelu_exact, pre_act)
    active = active_wide.astype(bf16)
    second_sum = (
        middle
        + jnp.dot(active, shrink_matrix, preferred_element_type=f32)
        + shrink_offset.astype(f32)
    )
    layer_out, second_back = jax.vjp(
        norm_rows, second_sum, second_scale.astype(f32), second_level.astype(f32)
    )
    grad_top = cotangent[0].astype(f32)
    grad_second, second_scale_grad, second_level_grad = second_back(grad_top)
    grad_ffn = grad_second.astype(bf16)
    shrink_grad = jnp.einsum("tf,td->fd", active, grad_ffn, preferred_element_type=f32)
    shrink_bias_grad = jnp.sum(grad_ffn.astype(f32), axis=0)
    grad_active = jnp.einsum("td,fd->tf", grad_ffn, shrink_matrix, preferred_element_type=f32)
    grad_pre = gelu_back(grad_active)[0].astype(bf16)
    expand_grad = jnp.einsum("td,tf->df", middle_low, grad_pre, preferred_element_type=f32)
    expand_bias_grad = jnp.sum(grad_pre.astype(f32), axis=0)
    grad_middle = grad_second + jnp.einsum(
        "tf,df->td", grad_pre, expand_matrix, preferred_element_type=f32
    )
    grad_first, first_scale_grad, first_level_grad = first_back(grad_middle)
    grad_branch = grad_first.astype(bf16)
    mixer_grad = jnp.einsum("td,te->de", attended, grad_branch, preferred_element_type=f32)
    mixer_bias_grad = jnp.sum(grad_branch.astype(f32), axis=0)
    grad_attended = jnp.einsum(
        "te,de->td", grad_branch, mixer_matrix, preferred_element_type=f32
    ).astype(bf16)
    grad_heads = lax.all_to_all(
        grad_attended.reshape(local_rows, head_count, head_slab),
        "head",
        split_axis=1,
        concat_axis=0,
        tiled=True,
    )
    grad_groups = grad_heads.reshape(group_count, group_blocks, BLOCK, group_heads, HEAD_DIM)

    def backward_group(pool_grad, scan_piece):
        group_piece, grad_group, lse_group = scan_piece
        scores, key_part, value_part = group_scores(pool_blocks, group_piece)
        soft_wide = jnp.exp(scores - lse_group[..., None])
        soft_low = soft_wide.astype(bf16)
        grad_soft = jnp.einsum(
            "gqhd,gnhd->ghqn", grad_group, value_part, preferred_element_type=f32
        )
        inner_sum = jnp.sum(grad_soft * soft_wide, axis=-1, keepdims=True)
        grad_scores = (soft_wide * (grad_soft - inner_sum) * score_scale).astype(bf16)
        flat_keys = key_part.reshape(group_blocks, -1, group_heads, HEAD_DIM)
        grad_query = jnp.einsum(
            "ghqn,gnhd->gqhd", grad_scores, flat_keys, preferred_element_type=f32
        )
        grad_key = jnp.einsum(
            "ghqn,gqhd->gnhd", grad_scores, group_piece[0], preferred_element_type=f32
        )
        grad_value = jnp.einsum("ghqn,gqhd->gnhd", soft_low, grad_group, preferred_element_type=f32)
        update = jnp.concatenate(
            [grad_key.reshape(-1, BLOCK, head_slab), grad_value.reshape(-1, BLOCK, head_slab)],
            axis=2,
        )
        pool_grad = pool_grad.at[group_piece[4].reshape(-1)].add(update)
        return (pool_grad, grad_query)

    pool_start = jnp.zeros((pool_count, BLOCK, 2 * head_slab), f32)
    pool_grad, grad_query_groups = lax.scan(
        backward_group, pool_start, (pieces, grad_groups, lse_groups)
    )
    sections = pool_grad.reshape(2 * reach_steps + 1, segment, 2 * head_slab)
    lower_total = sections[0]
    lower_total = (
        shifted(lower_total.astype(jnp.bfloat16), "blk", -1).astype(lower_total.dtype) + sections[1]
    )
    upper_total = sections[2 * reach_steps]
    upper_total = shifted(upper_total.astype(jnp.bfloat16), "blk", 1).astype(upper_total.dtype)
    pair_grad = (lower_total + upper_total).astype(bf16)
    query_grad_seg = grad_query_groups.reshape(segment, head_slab).astype(bf16)
    packed_grad = jnp.concatenate([query_grad_seg, pair_grad], axis=1).reshape(
        segment, 1, 3 * head_slab
    )
    token_grads = lax.all_to_all(packed_grad, "head", split_axis=0, concat_axis=1, tiled=True)
    grad_query_rows = token_grads[:, :, :head_slab].reshape(local_rows, model_width)
    grad_key_rows = token_grads[:, :, head_slab : 2 * head_slab].reshape(local_rows, model_width)
    grad_value_rows = token_grads[:, :, 2 * head_slab :].reshape(local_rows, model_width)
    query_grad = jnp.einsum("td,te->de", inputs, grad_query_rows, preferred_element_type=f32)
    query_bias_grad = jnp.sum(grad_query_rows.astype(f32), axis=0)
    key_grad = jnp.einsum("td,te->de", inputs, grad_key_rows, preferred_element_type=f32)
    value_grad = jnp.einsum("td,te->de", inputs, grad_value_rows, preferred_element_type=f32)
    value_bias_grad = jnp.sum(grad_value_rows.astype(f32), axis=0)
    input_grad = (
        grad_first
        + jnp.einsum("te,de->td", grad_query_rows, query_matrix, preferred_element_type=f32)
        + jnp.einsum("te,de->td", grad_key_rows, key_matrix, preferred_element_type=f32)
        + jnp.einsum("te,de->td", grad_value_rows, value_matrix, preferred_element_type=f32)
    )
    summed = (
        lax.psum_scatter(query_grad, ("head", "blk"), scatter_dimension=0, tiled=True),
        lax.psum_scatter(query_bias_grad, ("head", "blk"), scatter_dimension=0, tiled=True),
        lax.psum_scatter(key_grad, ("head", "blk"), scatter_dimension=0, tiled=True),
        lax.psum_scatter(value_grad, ("head", "blk"), scatter_dimension=0, tiled=True),
        lax.psum_scatter(value_bias_grad, ("head", "blk"), scatter_dimension=0, tiled=True),
        lax.psum_scatter(mixer_grad, ("head", "blk"), scatter_dimension=0, tiled=True),
        lax.psum_scatter(mixer_bias_grad, ("head", "blk"), scatter_dimension=0, tiled=True),
        lax.psum_scatter(first_scale_grad, ("head", "blk"), scatter_dimension=0, tiled=True),
        lax.psum_scatter(first_level_grad, ("head", "blk"), scatter_dimension=0, tiled=True),
        lax.psum_scatter(expand_grad, ("head", "blk"), scatter_dimension=0, tiled=True),
        lax.psum_scatter(expand_bias_grad, ("head", "blk"), scatter_dimension=0, tiled=True),
        lax.psum_scatter(shrink_grad, ("head", "blk"), scatter_dimension=0, tiled=True),
        lax.psum_scatter(shrink_bias_grad, ("head", "blk"), scatter_dimension=0, tiled=True),
        lax.psum_scatter(second_scale_grad, ("head", "blk"), scatter_dimension=0, tiled=True),
        lax.psum_scatter(second_level_grad, ("head", "blk"), scatter_dimension=0, tiled=True),
    )
    return (
        layer_out.astype(bf16)[None],
        input_grad[None],
        summed[0],
        summed[1],
        summed[2],
        summed[3],
        summed[4],
        summed[5],
        summed[6],
        summed[7],
        summed[8],
        summed[9],
        summed[10],
        summed[11],
        summed[12],
        summed[13],
        summed[14],
    )


def solution(mesh):
    in_specs = (
        P("blk", "head", None),
        P(("head", "blk"), None),
        P(("head", "blk")),
        P(("head", "blk"), None),
        P(("head", "blk"), None),
        P(("head", "blk")),
        P(("head", "blk"), None),
        P(("head", "blk")),
        P(("head", "blk")),
        P(("head", "blk")),
        P(("head", "blk"), None),
        P(("head", "blk")),
        P(("head", "blk"), None),
        P(("head", "blk")),
        P(("head", "blk")),
        P(("head", "blk")),
        P(),
        P("blk", None),
        P("blk", "head", None),
    )
    out_specs = (
        P("blk", "head", None),
        P("blk", "head", None),
        P(("head", "blk"), None),
        P(("head", "blk")),
        P(("head", "blk"), None),
        P(("head", "blk"), None),
        P(("head", "blk")),
        P(("head", "blk"), None),
        P(("head", "blk")),
        P(("head", "blk")),
        P(("head", "blk")),
        P(("head", "blk"), None),
        P(("head", "blk")),
        P(("head", "blk"), None),
        P(("head", "blk")),
        P(("head", "blk")),
        P(("head", "blk")),
    )
    return jax.shard_map(body, mesh=mesh, in_specs=in_specs, out_specs=out_specs, check_vma=False)
```

profile of v0, /device:TPU:0, one launch (start us, length us, event | category | flops | bytes accessed | tf_op | source)
XLA Modules:
  0.0 3872.8 jit_solution(12999597595795798904)
XLA Ops:
  24.0 42.6 %all-reduce.19 = (bf16[768]{0:T(1024)(128)(2,1)S(1)}, bf16[768]{0:T(1024)(128)(2,1)S(1)}, bf16[768]{0:T(1024)(128)(2,1)}, bf16[768]{0:T(1024)(128)(2,1)}, bf16[7...) all-reduce(bf16[768]{0:T(1024)(128)(2,1)S(1)} %dynamic-update-slice, ...), channel_id=1, replica_groups=mesh['head'=4,'blk'=8] {'head','blk'}, use_global_device_ids=true, to_apply=%add.1 | all-reduce | flops 9216 | bytes 36864
  71.6 53.5 %all-gather.11.cloned.1.call-done = bf16[768,768]{1,0:T(8,128)(2,1)} async-done(((bf16[24,768]{1,0:T(8,128)(2,1)}), bf16[768,768]{1,0:T(8,128)(2,1)}) %all-gather.11.cloned.1.call-update) | async-done | bytes 1179664 | tf_op jit(solution)/shard_map/all_gather | solution.py:139
  128.2 53.4 %all-gather.7.cloned.1.call-done = bf16[768,768]{1,0:T(8,128)(2,1)} async-done(((bf16[24,768]{1,0:T(8,128)(2,1)}), bf16[768,768]{1,0:T(8,128)(2,1)}) %all-gather.7.cloned.1.call-update) | async-done | bytes 1179664 | tf_op jit(solution)/shard_map/all_gather | solution.py:136
  194.6 55.0 %all-to-all-done = bf16[1024,4,576]{0,2,1:T(8,128)(2,1)} async-done(((bf16[1024,4,576]{0,2,1:T(8,128)(2,1)}), bf16[1024,4,576]{0,2,1:T(8,128)(2,1)}, u32[]{:S(2)}, u32[]{:S(2)}) %all-to-all-start) | async-done | bytes 4718624 | tf_op jit(solution)/shard_map/all_to_all | solution.py:186
  283.0 51.7 %collective-permute-done.1 = bf16[4096,384]{0,1:T(8,128)(2,1)} collective-permute-done((bf16[4096,384]{0,1:T(8,128)(2,1)S(1)}, bf16[4096,384]{0,1:T(8,128)(2,1)}, u32[]{:S(2)}, u32[]{:S(2)}) %collective-permute-start.1) | collective-permute-done | bytes 3145760 | tf_op jit(solution)/shard_map/ppermute | solution.py:22
  334.7 75.6 %collective-permute-done = bf16[4096,384]{0,1:T(8,128)(2,1)} collective-permute-done((bf16[4096,384]{0,1:T(8,128)(2,1)S(1)}, bf16[4096,384]{0,1:T(8,128)(2,1)}, u32[]{:S(2)}, u32[]{:S(2)}) %collective-permute-start) | collective-permute-done | bytes 3145760 | tf_op jit(solution)/shard_map/ppermute | solution.py:22
  418.7 12.6 copy.340
  431.3 657.0 %while.24 = (s32[]{:T(128)}, bf16[8,8,64,3,64]{2,4,3,1,0:T(8,128)(2,1)}, f32[8,8,3,64]{3,2,1,0:T(4,128)}, s32[8,8,12]{2,1,0:T(8,128)S(1)}, bf16[192,64,384]{2,1,...) while((s32[]{:T(128)}, ...), condition=%wide.region_19.20_spmd, body=%wide.region_16.19_spmd.sunk | while | flops 313890688 | bytes 107993600 | solution.py:259
  1095.6 17.0 reshape.896
  1113.2 23.6 reduce.9
  1148.2 16.8 all-to-all-done.1
  1189.2 38.1 multiply_convert_fusion.1
  1243.2 18.0 convert_reduce_fusion
  1281.9 20.0 all-to-all-done.2
  1315.4 1664.7 %while.25 = (s32[]{:T(128)}, f32[192,64,384]{2,1,0:T(8,128)}, bf16[8,8,64,3,64]{2,4,3,1,0:T(8,128)(2,1)}, s32[8,8,12]{2,1,0:T(8,128)}, bf16[8,8,64,3,64]{4,2,3,1...) while((s32[]{:T(128)}, f32[192,64,384]{2,1,0:T(8,128)}, ...), condition=%wide.region_31.32_spmd, body=%wide.region_28.31_spmd.sunk | while | flops 783298688 | bytes 283788128 | solution.py:339
  1406.4 16.2 fusion.201
  1422.6 17.6 fusion.200
  1469.4 12.7 pad_maximum_fusion.4
  1482.2 16.3 copy.431
  1498.5 23.7 scatter_fusion
  1590.5 12.5 copy.426
  1613.3 16.2 fusion.201
  1629.5 17.6 fusion.200
  1676.6 12.7 pad_maximum_fusion.4
  1689.3 16.3 copy.431
  1705.6 23.7 scatter_fusion
  1820.5 16.2 fusion.201
  1836.7 17.6 fusion.200
  1883.5 12.7 pad_maximum_fusion.4
  1896.2 16.3 copy.431
  1912.5 23.9 scatter_fusion
  2027.7 16.2 fusion.201
  2043.8 17.6 fusion.200
  2090.7 12.7 pad_maximum_fusion.4
  2103.4 16.3 copy.431
  2119.7 23.7 scatter_fusion
  2234.6 16.2 fusion.201
  2250.8 17.6 fusion.200
  2297.7 12.7 pad_maximum_fusion.4
  2310.4 16.3 copy.431
  2326.7 23.7 scatter_fusion
  2441.5 16.2 fusion.201
  2457.7 17.7 fusion.200
  2504.9 12.7 pad_maximum_fusion.4
  2517.6 16.3 copy.431
  2533.9 23.8 scatter_fusion
  2649.0 16.2 fusion.201
  2665.1 17.6 fusion.200
  2711.9 12.7 pad_maximum_fusion.4
  2724.7 16.3 copy.431
  2741.0 23.8 scatter_fusion
  2856.0 16.2 fusion.201
  2872.1 17.6 fusion.200
  2919.0 12.7 pad_maximum_fusion.4
  2931.7 16.3 copy.431
  2948.0 23.9 scatter_fusion
  3017.3 113.6 %collective-permute-done.3 = bf16[4096,384]{1,0:T(8,128)(2,1)} collective-permute-done((bf16[4096,384]{1,0:T(8,128)(2,1)}, bf16[4096,384]{1,0:T(8,128)(2,1)}, u32[]{:S(2)}, u32[]{:S(2)}) %collective-permute-start.3) | collective-permute-done | bytes 3145760 | tf_op jit(solution)/shard_map/ppermute | solution.py:22
  3165.9 50.8 %all-to-all-done.3 = bf16[4,2,294912]{2,1,0:T(2,128)(2,1)} async-done(((bf16[4,2,294912]{2,1,0:T(2,128)(2,1)}), bf16[4,2,294912]{2,1,0:T(2,128)(2,1)}, u32[]{:S(2)}, u32[]{:S(2)}) %all-to-all-start.3) | async-done | bytes 4718624 | tf_op jit(solution)/shard_map/all_to_all | solution.py:354
  3301.1 41.0 %all-reduce.18 = (f32[768]{0:T(1024)S(1)}, f32[768]{0:T(1024)S(1)}, f32[768]{0:T(1024)S(1)}, f32[768]{0:T(1024)S(1)}, f32[768]{0:T(1024)S(1)}, /*index=5*/f32[30...) all-reduce(f32[768]{0:T(1024)S(1)} %reduce_sum.236, ...), channel_id=3, replica_groups=mesh['head'=4,'blk'=8] {'head','blk'}, use_global_device_ids=true, to_apply=%region_34.35.clone | all-reduce | flops 9216 | bytes 73728
  3355.6 18.0 reduce-scatter.19.cloned.1.call-done
  3373.7 104.0 %reduce-scatter.23.cloned.1.call-done = f32[24,768]{1,0:T(8,128)} async-done(((f32[768,768]{1,0:T(8,128)}), f32[24,768]{1,0:T(8,128)}) %reduce-scatter.23.cloned.1.call-update) | async-done | bytes 73744
  3477.7 104.6 %reduce-scatter.21.cloned.1.call-done = f32[24,768]{1,0:T(8,128)} async-done(((f32[768,768]{1,0:T(8,128)}), f32[24,768]{1,0:T(8,128)}) %reduce-scatter.21.cloned.1.call-update) | async-done | bytes 73744
  3582.3 141.1 %reduce-scatter.15.cloned.1.call-done = f32[24,3072]{1,0:T(8,128)} async-done(((f32[768,3072]{1,0:T(8,128)}), f32[24,3072]{1,0:T(8,128)}) %reduce-scatter.15.cloned.1.call-update) | async-done | bytes 294928 | tf_op jit(solution)/shard_map/reduce_scatter | solution.py:379
  3723.4 142.1 %reduce-scatter.17.cloned.1.call-done = f32[96,768]{1,0:T(8,128)} async-done(((f32[3072,768]{1,0:T(8,128)}), f32[96,768]{1,0:T(8,128)}) %reduce-scatter.17.cloned.1.call-update) | async-done | bytes 294928 | tf_op jit(solution)/shard_map/reduce_scatter | solution.py:381
  (871 shorter events, 1946.5 us)
Async XLA Ops:
  7.2 61.2 %all-gather.9.cloned.1.call-start = ((), (), s32[]{:S(2)}) async-start(), calls=%async_computation.11 | async-start | bytes 1216512 | tf_op jit(solution)/shard_map/all_gather | solution.py:138
  8.8 116.3 %all-gather.11.cloned.1.call-start = ((), (), s32[]{:S(2)}) async-start(), calls=%async_computation.12 | async-start | bytes 1216512 | tf_op jit(solution)/shard_map/all_gather | solution.py:139
  10.3 171.3 %all-gather.7.cloned.1.call-start = ((), (), s32[]{:S(2)}) async-start(), calls=%async_computation.10 | async-start | bytes 1216512 | tf_op jit(solution)/shard_map/all_gather | solution.py:136
  11.9 1171.3 %all-gather.13.cloned.1.call-start = ((), (), s32[]{:S(2)}) async-start(), calls=%async_computation.13 | async-start | bytes 1216512 | tf_op jit(solution)/shard_map/all_gather | solution.py:141
  13.5 1175.7 %all-gather.15.cloned.1.call-start = ((), (), s32[]{:S(2)}) async-start(), calls=%async_computation.14 | async-start | bytes 4866048 | tf_op jit(solution)/shard_map/all_gather | solution.py:145
  187.2 6.6 copy-start.44
  187.2 6.7 copy-start.54
  187.2 62.4 %all-to-all-start = ((bf16[1024,4,576]{0,2,1:T(8,128)(2,1)}), bf16[1024,4,576]{0,2,1:T(8,128)(2,1)}, u32[]{:S(2)}, u32[]{:S(2)}) async-start(bf16[1024,4,576]{0,2,1:T(8,128)(2,1)} %pad_maximum_fusion.2), calls=%async_computation | async-start | bytes 9437184 | tf_op jit(solution)/shard_map/all_to_all | solution.py:186
  260.9 73.8 %collective-permute-start.1 = (bf16[4096,384]{0,1:T(8,128)(2,1)S(1)}, bf16[4096,384]{0,1:T(8,128)(2,1)}, u32[]{:S(2)}, u32[]{:S(2)}) collective-permute-start(bf16[4096,384]{0,1:T(8,128)(2,1)S(1)} %slice.153), channel_id=1, source_target_pairs={{1,0},{2,1},{3,2},{4,3},{5,4},{6,5},{7,6},{9,8},{10,9},{11,10},{12... | collective-permute-start | bytes 9437192 | tf_op jit(solution)/shard_map/ppermute | solution.py:22
  262.2 148.1 %collective-permute-start = (bf16[4096,384]{0,1:T(8,128)(2,1)S(1)}, bf16[4096,384]{0,1:T(8,128)(2,1)}, u32[]{:S(2)}, u32[]{:S(2)}) collective-permute-start(bf16[4096,384]{0,1:T(8,128)(2,1)S(1)} %slice.153), channel_id=1, source_target_pairs={{0,1},{1,2},{2,3},{3,4},{4,5},{5,6},{6,7},{8,9},{9,10},{10,11},{11... | collective-permute-start | bytes 9437192 | tf_op jit(solution)/shard_map/ppermute | solution.py:22
  1088.3 7.3 copy-start.2
  1088.3 7.3 copy-start.34
  1088.3 7.3 copy-start.35
  1088.4 7.2 copy-start.36
  1088.4 7.2 copy-start.37
  1088.4 7.2 copy-start.38
  1088.4 7.2 copy-start.39
  1136.8 7.2 copy-start.33
  1140.2 6.2 copy-start.64
  1140.2 6.2 copy-start.63
  1140.2 6.2 copy-start.62
  1140.2 6.2 copy-start.61
  1140.2 6.2 copy-start.60
  1140.2 6.2 copy-start.59
  1140.2 6.2 copy-start.53
  1140.2 24.8 all-to-all-start.1
  1143.9 83.4 %all-gather.17.cloned.1.call-start = ((), (), s32[]{:S(2)}) async-start(), calls=%async_computation.15 | async-start | bytes 4866048 | tf_op jit(solution)/shard_map/all_gather | solution.py:147
  1146.3 126.4 %copy-start.45 = (f32[768]{0:T(1024)}, f32[768]{0:T(1024)S(1)}, u32[]{:S(2)}) copy-start(f32[768]{0:T(1024)S(1)} %convert_element_type.189) | copy-start | bytes 9220
  1146.4 81.0 %copy-start.55 = (f32[768]{0:T(1024)}, f32[768]{0:T(1024)S(1)}, u32[]{:S(2)}) copy-start(f32[768]{0:T(1024)S(1)} %convert_element_type.191) | copy-start | bytes 9220
  1148.2 113.1 %copy-start.7 = (bf16[1,1024,768]{1,2,0:T(8,128)(2,1)}, bf16[1,1024,768]{1,2,0:T(8,128)(2,1)S(1)}, u32[]{:S(2)}) copy-start(bf16[1,1024,768]{1,2,0:T(8,128)(2,1)S(1)} %copy.350) | copy-start | bytes 4718596
  1187.2 85.6 %copy-start.42 = (f32[1024]{0:T(1024)}, f32[1024]{0:T(1024)S(1)}, u32[]{:S(2)}) copy-start(f32[1024]{0:T(1024)S(1)} %broadcast_multiply_fusion.1) | copy-start | bytes 12292
  1189.2 83.6 %copy-start.47 = (f32[1024]{0:T(1024)}, f32[1024]{0:T(1024)S(1)}, u32[]{:S(2)}) copy-start(f32[1024]{0:T(1024)S(1)} %fusion.98) | copy-start | bytes 12292
  1243.2 18.1 copy-start.28
  1261.3 11.5 copy-start.13
  1278.3 23.6 all-to-all-start.2
  1306.5 8.8 copy-start.3
  1371.6 8.4 copy-start.5
  1396.1 10.3 copy-start.6
  1578.4 8.4 copy-start.5
  1603.0 10.3 copy-start.6
  1785.3 8.4 copy-start.5
  1810.0 10.5 copy-start.6
  1992.6 8.4 copy-start.5
  2017.4 10.3 copy-start.6
  2199.8 8.4 copy-start.5
  2224.3 10.3 copy-start.6
  2406.6 8.4 copy-start.5
  2431.2 10.3 copy-start.6
  2613.8 8.4 copy-start.5
  2638.4 10.5 copy-start.6
  2820.8 8.4 copy-start.5
  2845.7 10.3 copy-start.6
  2991.1 139.9 %collective-permute-start.3 = (bf16[4096,384]{1,0:T(8,128)(2,1)}, bf16[4096,384]{1,0:T(8,128)(2,1)}, u32[]{:S(2)}, u32[]{:S(2)}) collective-permute-start(bf16[4096,384]{1,0:T(8,128)(2,1)} %bitcast.62), channel_id=1, source_target_pairs={{0,1},{1,2},{2,3},{3,4},{4,5},{5,6},{6,7},{8,9},{9,10},{10,11},{11... | collective-permute-start | bytes 9437192 | tf_op jit(solution)/shard_map/ppermute | solution.py:22
  2997.7 7.7 copy-start.18
  2997.7 133.2 %collective-permute-start.2 = (bf16[4096,384]{1,0:T(8,128)(2,1)}, bf16[4096,384]{1,0:T(8,128)(2,1)}, u32[]{:S(2)}, u32[]{:S(2)}) collective-permute-start(bf16[4096,384]{1,0:T(8,128)(2,1)} %bitcast.60), channel_id=1, source_target_pairs={{1,0},{2,1},{3,2},{4,3},{5,4},{6,5},{7,6},{9,8},{10,9},{11,10},{12... | collective-permute-start | bytes 9437192 | tf_op jit(solution)/shard_map/ppermute | solution.py:22
  3157.6 59.1 %all-to-all-start.3 = ((bf16[4,2,294912]{2,1,0:T(2,128)(2,1)}), bf16[4,2,294912]{2,1,0:T(2,128)(2,1)}, u32[]{:S(2)}, u32[]{:S(2)}) async-start(bf16[4,2,294912]{2,1,0:T(2,128)(2,1)} %reshape.914), calls=%async_computation.3 | async-start | bytes 9437184 | tf_op jit(solution)/shard_map/all_to_all | solution.py:354
  3162.8 192.8 %reduce-scatter.13.cloned.1.call-start = ((), (), s32[]{:S(2)}) async-start(), calls=%async_computation.16 | async-start | bytes 2433024 | tf_op jit(solution)/shard_map/reduce_scatter | solution.py:375
  3165.8 207.8 %reduce-scatter.19.cloned.1.call-start = ((), (), s32[]{:S(2)}) async-start(), calls=%async_computation.19 | async-start | bytes 2433024
  3255.8 221.9 %reduce-scatter.23.cloned.1.call-start = ((), (), s32[]{:S(2)}) async-start(), calls=%async_computation.21 | async-start | bytes 2433024
  3263.5 318.8 %reduce-scatter.21.cloned.1.call-start = ((), (), s32[]{:S(2)}) async-start(), calls=%async_computation.20 | async-start | bytes 2433024
  3271.3 452.1 %reduce-scatter.15.cloned.1.call-start = ((), (), s32[]{:S(2)}) async-start(), calls=%async_computation.17 | async-start | bytes 9732096 | tf_op jit(solution)/shard_map/reduce_scatter | solution.py:379
  3282.2 583.3 %reduce-scatter.17.cloned.1.call-start = ((), (), s32[]{:S(2)}) async-start(), calls=%async_computation.18 | async-start | bytes 9732096 | tf_op jit(solution)/shard_map/reduce_scatter | solution.py:381
  3295.8 50.9 %copy-start.25 = (bf16[1024,4,192]{0,2,1:T(8,128)(2,1)S(1)}, bf16[1024,4,192]{0,2,1:T(8,128)(2,1)}, u32[]{:S(2)}) copy-start(bf16[1024,4,192]{0,2,1:T(8,128)(2,1)} %copy-done.24) | copy-start | bytes 4718596
  3297.4 49.4 %copy-start.66 = (bf16[768,768]{1,0:T(8,128)(2,1)S(1)}, bf16[768,768]{1,0:T(8,128)(2,1)}, u32[]{:S(2)}) copy-start(bf16[768,768]{1,0:T(8,128)(2,1)} %all-gather.7.cloned.1.call-done) | copy-start | bytes 3538948
  (59 other events, 208.6 us)
Sparse Core Ops, SparseCore 0:
  11.5 56.8 all-gather.8
  71.9 53.1 all-gather.10
  128.5 53.0 all-gather.6
  185.0 55.2 all-gather.12
  243.6 135.9 all-gather.14
  1147.9 63.7 all-gather.16
  3169.5 99.2 reduce-scatter.12
  3275.5 98.1 reduce-scatter.18
  3379.5 98.0 reduce-scatter.22
  3484.2 98.0 reduce-scatter.20
  3588.8 134.6 reduce-scatter.14
  3730.8 134.6 reduce-scatter.16
where the time goes:
time: 3900 us; the launch traced here: 3870 us
  local copies, waits for them, and re-layouts  1660 us (43%)
  waiting for transfers between devices  1000 us (26%)
  matrix products  575 us (15%)
  other arithmetic  489 us (13%)
  blocking collectives  83.6 us (2%)
    gather x32, local copies, waits for them, and re-layouts, group_scores(): fetched = pool_now[group_local]  270 us
    ppermute x4, waiting for transfers between devices, shifted(): return lax.ppermute(array, axis, pairs)  241 us
    unnamed x15, waiting for transfers between devices  227 us
    scatter-add x8, other arithmetic, backward_group(): pool_grad = pool_grad.at[group_piece[4].reshape(-1)].add(update)  190 us
    slice x24, local copies, waits for them, and re-layouts, group_scores(): fetched[..., head_slab:].reshape(group_blocks, -1, group_heads, HEAD_DIM)  177 us
    reshape x16, local copies, waits for them, and re-layouts, group_scores(): scores.reshape(group_blocks, group_heads, BLOCK, -1)  148 us
    reduce_scatter x1, waiting for transfers between devices, body(): lax.psum_scatter(shrink_grad, ('head', 'blk'), scatter_dimension=0, tiled...  142 us
    reduce_scatter x1, waiting for transfers between devices, body(): lax.psum_scatter(expand_grad, ('head', 'blk'), scatter_dimension=0, tiled...  141 us
  transfers between devices with their start and end apart: 20, of which 15 were waited for; matrix products, arithmetic and copies ran while one was open for 24% of the time, Pallas kernels for 0%

commit v1 on v0

v1 whole, which is shorter than its diff:
```python
import functools
import math

import jax
import jax.numpy as jnp
from jax import lax
from jax.experimental import pallas as pl
from jax.experimental.pallas import tpu as pltpu
from jax.sharding import PartitionSpec as P

HEADS = 12
HEAD_DIM = 64
BLOCK = 64
GLOBAL_BLOCKS = 2
MAXDOC = 4096
VMEM_BYTES = 60 * 2**20

layer_eps = 1e-12
masked_score = -1e30

def chunk_tile(rows, width):
    return lax.broadcasted_iota(jnp.int32, (rows, width), 1) // HEAD_DIM


def head_diag(tile, heads):
    owner = chunk_tile(BLOCK, heads * HEAD_DIM)
    return jnp.concatenate(
        [jnp.where(owner == head, tile, jnp.zeros_like(tile)) for head in range(heads)], axis=0
    )


def diag_rows(full, heads):
    owner = chunk_tile(BLOCK, heads * HEAD_DIM)
    picked = full[:BLOCK]
    for head in range(1, heads):
        picked = jnp.where(owner == head, full[head * BLOCK : (head + 1) * BLOCK], picked)
    return picked


def tile_bias(block, count, slots, place_ref, base_ref, kind_ref, first_ref, end_ref):
    first = first_ref[pl.ds(block, 1), :]
    end = end_ref[pl.ds(block, 1), :]
    key = lax.broadcasted_iota(jnp.int32, (BLOCK, 2 * BLOCK), 0)
    starts = []
    biases = []
    for slot in range(count):
        entry = block * slots + slot
        starts.append(pl.multiple_of(place_ref[entry] * BLOCK, BLOCK))
        base = base_ref[entry]
        kind = kind_ref[entry]
        high = jnp.where(kind == 2, end, first + GLOBAL_BLOCKS * BLOCK)
        high = jnp.where(kind == 0, -1, high - base)
        allowed = (key >= first - base) & (key < high)
        biases.append(jnp.where(allowed, 0.0, masked_score))
    return starts, jnp.concatenate(biases, axis=0)


NT = (((1,), (1,)), ((), ()))
NN = (((1,), (0,)), ((), ()))
TN = (((0,), (0,)), ((), ()))


def soft_columns(keys, query_diag, bias, heads):
    scores = lax.dot_general(keys, query_diag, NT, preferred_element_type=jnp.float32)
    scores = scores + jnp.concatenate([bias] * (heads // 2), axis=1)
    top = jnp.max(scores, axis=0, keepdims=True)
    raised = jnp.exp(scores - top)
    total = jnp.sum(raised, axis=0, keepdims=True)
    return raised * (1.0 / total)


def load_pool(chunks, pool_ref, sems):
    rows = chunks[0].shape[0]
    copies = [
        pltpu.make_async_copy(chunk, pool_ref.at[pl.ds(n * rows, rows)], sems.at[n])
        for n, chunk in enumerate(chunks)
    ]
    for copy in copies:
        copy.start()
    return copies


def attend_kernel(sizes, *refs):
    blocks, slots, few, groups, width = sizes
    place_ref, base_ref, kind_ref, count_ref, first_ref, end_ref, query_ref = refs[:7]
    chunks = refs[7:-3]
    out_ref, pool_ref, sems = refs[-3:]
    for copy in load_pool(chunks, pool_ref, sems):
        copy.wait()

    def work(block, count):
        starts, bias = tile_bias(
            block, count, slots, place_ref, base_ref, kind_ref, first_ref, end_ref
        )
        here = pl.ds(pl.multiple_of(block * BLOCK, BLOCK), BLOCK)
        for low, heads in groups:
            span = heads * HEAD_DIM
            keys = jnp.concatenate(
                [pool_ref[pl.ds(start, BLOCK), low : low + span] for start in starts], axis=0
            )
            values = jnp.concatenate(
                [
                    pool_ref[pl.ds(start, BLOCK), width + low : width + low + span]
                    for start in starts
                ],
                axis=0,
            )
            query_diag = head_diag(query_ref[here, low : low + span], heads)
            probs = soft_columns(keys, query_diag, bias, heads).astype(jnp.bfloat16)
            mixed = lax.dot_general(probs, values, TN, preferred_element_type=jnp.float32)
            out_ref[here, low : low + span] = diag_rows(mixed, heads).astype(jnp.bfloat16)

    def step(block, carry):
        short = count_ref[block] <= few

        @pl.when(short)
        def _():
            work(block, few)

        @pl.when(jnp.logical_not(short))
        def _():
            work(block, slots)

        return carry

    lax.fori_loop(0, blocks, step, 0)


def attend_back_kernel(sizes, *refs):
    blocks, slots, few, groups, width, parts = sizes
    place_ref, base_ref, kind_ref, count_ref, first_ref, end_ref, query_ref, grad_ref = refs[:8]
    chunks = refs[8 : 8 + parts]
    query_grad_ref = refs[8 + parts]
    outs = refs[9 + parts : 9 + 2 * parts]
    pool_ref, total_ref, sems = refs[9 + 2 * parts :]
    copies = load_pool(chunks, pool_ref, sems)
    rows = chunks[0].shape[0]
    strip = 128

    def clear(n, carry):
        at = pl.ds(pl.multiple_of(n * strip, strip), strip)
        total_ref[at, :] = jnp.zeros((strip, 2 * width), jnp.float32)
        return carry

    lax.fori_loop(0, parts * rows // strip, clear, 0)
    for copy in copies:
        copy.wait()

    def work(block, count):
        starts, bias = tile_bias(
            block, count, slots, place_ref, base_ref, kind_ref, first_ref, end_ref
        )
        here = pl.ds(pl.multiple_of(block * BLOCK, BLOCK), BLOCK)
        for low, heads in groups:
            span = heads * HEAD_DIM
            keys = jnp.concatenate(
                [pool_ref[pl.ds(start, BLOCK), low : low + span] for start in starts], axis=0
            )
            values = jnp.concatenate(
                [
                    pool_ref[pl.ds(start, BLOCK), width + low : width + low + span]
                    for start in starts
                ],
                axis=0,
            )
            query_diag = head_diag(query_ref[here, low : low + span], heads)
            grad_diag = head_diag(grad_ref[here, low : low + span], heads)
            probs = soft_columns(keys, query_diag, bias, heads)
            grad_probs = lax.dot_general(values, grad_diag, NT, preferred_element_type=jnp.float32)
            inner = jnp.sum(probs * grad_probs, axis=0, keepdims=True)
            grad_scores = (probs * (grad_probs - inner)).astype(jnp.bfloat16)
            grad_values = lax.dot_general(
                probs.astype(jnp.bfloat16), grad_diag, NN, preferred_element_type=jnp.float32
            )
            grad_keys = lax.dot_general(
                grad_scores, query_diag, NN, preferred_element_type=jnp.float32
            )
            grad_query = lax.dot_general(grad_scores, keys, TN, preferred_element_type=jnp.float32)
            query_grad_ref[here, low : low + span] = (
                diag_rows(grad_query, heads) * HEAD_DIM**-0.5
            ).astype(jnp.bfloat16)
            for slot, start in enumerate(starts):
                lines = slice(slot * BLOCK, (slot + 1) * BLOCK)
                total_ref[pl.ds(start, BLOCK), low : low + span] += grad_keys[lines]
                total_ref[pl.ds(start, BLOCK), width + low : width + low + span] += grad_values[
                    lines
                ]

    def step(block, carry):
        short = count_ref[block] <= few

        @pl.when(short)
        def _():
            work(block, few)

        @pl.when(jnp.logical_not(short))
        def _():
            work(block, slots)

        return carry

    lax.fori_loop(0, blocks, step, 0)

    def lower(n, carry):
        at = pl.ds(pl.multiple_of(n * strip, strip), strip)
        pool_ref[at, :] = total_ref[at, :].astype(jnp.bfloat16)
        return carry

    sends = []
    for n, out in enumerate(outs):
        lax.fori_loop(n * rows // strip, (n + 1) * rows // strip, lower, 0)
        send = pltpu.make_async_copy(pool_ref.at[pl.ds(n * rows, rows)], out, sems.at[n])
        send.start()
        sends.append(send)
    for send in sends:
        send.wait()


def attend(lists, query_rows, chunks, groups, slots, few):
    tokens, width = query_rows.shape
    rows = chunks[0].shape[0]
    parts = len(chunks)
    blocks = tokens // BLOCK
    smem = pl.BlockSpec(memory_space=pltpu.SMEM)
    vmem = pl.BlockSpec(memory_space=pltpu.VMEM)
    hbm = pl.BlockSpec(memory_space=pl.ANY)
    keys = few * BLOCK
    return pl.pallas_call(
        functools.partial(attend_kernel, (blocks, slots, few, groups, width)),
        out_shape=jax.ShapeDtypeStruct((tokens, width), jnp.bfloat16),
        in_specs=[smem] * 4 + [vmem] * 3 + [hbm] * parts,
        out_specs=vmem,
        scratch_shapes=[
            pltpu.VMEM((parts * rows, 2 * width), jnp.bfloat16),
            pltpu.SemaphoreType.DMA((parts,)),
        ],
        compiler_params=pltpu.CompilerParams(vmem_limit_bytes=VMEM_BYTES),
        cost_estimate=pl.CostEstimate(
            flops=16 * tokens * keys * width,
            bytes_accessed=4 * parts * rows * width,
            transcendentals=tokens * keys * width // HEAD_DIM,
        ),
        name="attend",
    )(*lists, query_rows, *chunks)


def attend_back(lists, query_rows, grad_rows, chunks, groups, slots, few):
    tokens, width = query_rows.shape
    rows = chunks[0].shape[0]
    parts = len(chunks)
    blocks = tokens // BLOCK
    smem = pl.BlockSpec(memory_space=pltpu.SMEM)
    vmem = pl.BlockSpec(memory_space=pltpu.VMEM)
    hbm = pl.BlockSpec(memory_space=pl.ANY)
    keys = few * BLOCK
    return pl.pallas_call(
        functools.partial(attend_back_kernel, (blocks, slots, few, groups, width, parts)),
        out_shape=[jax.ShapeDtypeStruct((tokens, width), jnp.bfloat16)]
        + [jax.ShapeDtypeStruct((rows, 2 * width), jnp.bfloat16)] * parts,
        in_specs=[smem] * 4 + [vmem] * 4 + [hbm] * parts,
        out_specs=[vmem] + [hbm] * parts,
        scratch_shapes=[
            pltpu.VMEM((parts * rows, 2 * width), jnp.bfloat16),
            pltpu.VMEM((parts * rows, 2 * width), jnp.float32),
            pltpu.SemaphoreType.DMA((parts,)),
        ],
        compiler_params=pltpu.CompilerParams(vmem_limit_bytes=VMEM_BYTES),
        cost_estimate=pl.CostEstimate(
            flops=40 * tokens * keys * width,
            bytes_accessed=8 * parts * rows * width,
            transcendentals=tokens * keys * width // HEAD_DIM,
        ),
        name="attend_back",
    )(*lists, query_rows, grad_rows, *chunks)


def token_docs(positions, starts):
    before = starts[None, :] <= positions[:, None]
    return jnp.max(jnp.where(before, starts[None, :], 0), axis=1)


def token_ends(positions, starts, tokens):
    after = starts[None, :] > positions[:, None]
    return jnp.min(jnp.where(after, starts[None, :], tokens), axis=1)


def block_lists(block_ids, random_picks, starts, total_blocks):
    lead_tokens = block_ids * BLOCK
    first_lead = token_docs(lead_tokens, starts)
    first_tail = token_docs(lead_tokens + BLOCK - 1, starts)
    end_tail = token_ends(lead_tokens + BLOCK - 1, starts, total_blocks * BLOCK)
    columns = [block_ids - 1, block_ids, block_ids + 1]
    columns += [random_picks[:, pick] for pick in range(random_picks.shape[1])]
    for anchor in (first_lead, first_tail):
        columns += [anchor // BLOCK + offset for offset in range(GLOBAL_BLOCKS + 1)]
    candidate = jnp.clip(jnp.stack(columns, axis=1), 0, total_blocks - 1)
    repeats = [jnp.zeros(candidate.shape[:1], dtype=jnp.bool_)]
    for column in range(1, candidate.shape[1]):
        repeats.append(jnp.any(candidate[:, :column] == candidate[:, column : column + 1], axis=1))
    distinct = jnp.logical_not(jnp.stack(repeats, axis=1))
    nearby = jnp.logical_or(
        jnp.abs(candidate - block_ids[:, None]) <= 1,
        jnp.any(candidate[:, :, None] == random_picks[:, None, :], axis=2),
    )
    lead = candidate * BLOCK
    reached = (lead + BLOCK > first_lead[:, None]) & (lead < end_tail[:, None])
    reached &= nearby | (lead < first_tail[:, None] + GLOBAL_BLOCKS * BLOCK)
    return candidate, distinct & reached, nearby


def norm_rows(values_in, gain_row, shift_row):
    row_mean = jnp.mean(values_in, axis=-1, keepdims=True)
    centred = values_in - row_mean
    spread = jnp.mean(centred * centred, axis=-1, keepdims=True)
    return centred * lax.rsqrt(spread + layer_eps) * gain_row + shift_row


def gelu_exact(values_in):
    return jax.nn.gelu(values_in, approximate=False)


def pick(flag, first, second):
    return jnp.where(flag == 0, first, second)


def split_low(wide, width):
    high = lax.reduce_precision(wide, 8, 7)
    parts = [high.astype(jnp.bfloat16), (wide - high).astype(jnp.bfloat16)]
    pad = width - 2 * wide.shape[-1]
    parts.append(jnp.zeros(wide.shape[:-1] + (pad,), jnp.bfloat16))
    return jnp.concatenate(parts, axis=-1)


def join_low(packed, count):
    wide = packed.astype(jnp.float32)
    return wide[..., :count] + wide[..., count : 2 * count]


def body(
    tokens_in,
    query_weight,
    query_bias,
    key_weight,
    value_weight,
    value_bias,
    mixer_weight,
    mixer_bias,
    first_gain,
    first_shift,
    expand_weight,
    expand_bias,
    shrink_weight,
    shrink_bias,
    second_gain,
    second_shift,
    doc_starts,
    random_blocks,
    cotangent,
):
    f32 = jnp.float32
    bf16 = jnp.bfloat16
    axes = ("head", "blk")
    head_count = lax.axis_size("head")
    cycle_size = lax.axis_size("blk")
    devices = head_count * cycle_size
    head_index = lax.axis_index("head")
    cycle_index = lax.axis_index("blk")
    side = head_index // 2
    core = head_index % 2
    local_rows = tokens_in.shape[1]
    model_width = tokens_in.shape[2]
    half_width = model_width // 2
    hidden = expand_weight.shape[1]
    fold = hidden // model_width
    own_rows = query_weight.shape[0]
    part_blocks = local_rows // BLOCK
    half_blocks = 2 * part_blocks
    total_blocks = part_blocks * devices
    slots = 3 + random_blocks.shape[1] + 2 * (GLOBAL_BLOCKS + 1)
    few = slots - GLOBAL_BLOCKS - 1
    groups = ((0, 4), (4 * HEAD_DIM, 2))

    def flat(head, cycle):
        return head * cycle_size + cycle

    everywhere = [(h, b) for h in range(head_count) for b in range(cycle_size)]
    over_side = [(flat(h, b), flat(h ^ 2, b)) for h, b in everywhere]
    over_core = [(flat(h, b), flat(h ^ 1, b)) for h, b in everywhere]
    inward = [
        (flat(h, b), flat(h, b + (1 if h >= 2 else -1)))
        for h, b in everywhere
        if 0 <= b + (1 if h >= 2 else -1) < cycle_size
    ]
    outward = [
        (flat(h, b), flat(h, b + (-1 if h >= 2 else 1)))
        for h, b in everywhere
        if 0 <= b + (-1 if h >= 2 else 1) < cycle_size
    ]

    def send(array, pairs):
        return lax.ppermute(array, axes, pairs)

    def send_back(array, pairs):
        return lax.ppermute(array, axes, [(b, a) for a, b in pairs])

    inputs = tokens_in[0]
    beside = send(inputs, over_side)
    near = send(inputs, inward)
    passed = send(near, over_side)
    far = send(inputs, outward)
    held = [inputs, beside, near, passed, far]

    low_query = query_weight.astype(bf16)
    low_key = key_weight.astype(bf16)
    low_value = value_weight.astype(bf16)
    vectors = [
        query_bias,
        value_bias,
        mixer_bias,
        first_gain,
        first_shift,
        shrink_bias,
        second_gain,
        second_shift,
    ]
    lines = [vector[:, None] for vector in vectors] + [expand_bias.reshape(own_rows, fold)]
    line_count = len(vectors) + fold
    line_width = 128
    lines.append(jnp.zeros((own_rows, line_width - line_count), f32))
    shard = jnp.concatenate(
        [
            low_key[:, :half_width],
            low_value[:, :half_width],
            low_query[:, :half_width],
            low_key[:, half_width:],
            low_value[:, half_width:],
            low_query[:, half_width:],
            jnp.concatenate(lines, axis=1).astype(bf16),
        ],
        axis=1,
    )
    trio = 3 * half_width
    spread = jnp.broadcast_to(shard[None], (cycle_size,) + shard.shape)
    column = lax.all_to_all(spread, "blk", split_axis=0, concat_axis=0, tiled=True)
    column = column.reshape(cycle_size * own_rows, -1)
    column_beside = send(column, over_side)
    pair = pick(side, jnp.stack([column, column_beside]), jnp.stack([column_beside, column]))
    wanted = jnp.concatenate(
        [pick(core, pair[..., :trio], pair[..., trio : 2 * trio]), pair[..., 2 * trio :]], axis=2
    )
    unwanted = jnp.concatenate(
        [pick(core, pair[..., trio : 2 * trio], pair[..., :trio]), pair[..., 2 * trio :]], axis=2
    )
    given = send(unwanted, over_core)
    table = pick(core, jnp.stack([wanted, given], axis=1), jnp.stack([given, wanted], axis=1))
    table = table.reshape(model_width, trio + line_width)
    pair_matrix = table[:, :model_width]
    query_matrix = table[:, model_width:trio]
    vector_rows = table[:, trio : trio + line_count].astype(f32).T
    query_offset = pick(core, vector_rows[0, :half_width], vector_rows[0, half_width:])
    value_offset = pick(core, vector_rows[1, :half_width], vector_rows[1, half_width:])
    mixer_offset, first_scale, first_level, shrink_offset, second_scale, second_level = [
        vector_rows[n] for n in range(2, len(vectors))
    ]
    expand_offset = table[:, trio + len(vectors) : trio + line_count].astype(f32).reshape(hidden)
    pair_offset = jnp.concatenate([jnp.zeros((half_width,), f32), value_offset])

    bundle = jnp.concatenate(
        [
            expand_weight.astype(bf16).reshape(own_rows * fold, model_width),
            shrink_weight.astype(bf16),
            mixer_weight.astype(bf16),
        ],
        axis=0,
    )
    wide_rows = own_rows * fold
    bundles = lax.all_gather(bundle, axes, axis=0, tiled=True).reshape(
        devices, bundle.shape[0], model_width
    )
    expand_matrix = bundles[:, :wide_rows].reshape(model_width, hidden)
    shrink_matrix = bundles[:, wide_rows : 2 * wide_rows].reshape(hidden, model_width)
    mixer_matrix = bundles[:, 2 * wide_rows :].reshape(model_width, model_width)

    half_index = 2 * cycle_index + side
    block_of = jnp.arange(half_blocks, dtype=jnp.int32)
    part_of = jnp.where(block_of < part_blocks, core, 1 - core)
    block_ids = half_index * half_blocks + part_of * part_blocks + block_of % part_blocks
    picks = jnp.concatenate(
        [
            lax.dynamic_slice_in_dim(random_blocks, head_index * part_blocks, part_blocks),
            lax.dynamic_slice_in_dim(random_blocks, (head_index ^ 1) * part_blocks, part_blocks),
        ],
        axis=0,
    )
    candidate, useful, nearby = block_lists(block_ids, picks, doc_starts, total_blocks)
    apart = candidate // half_blocks - half_index
    reach = jnp.abs(apart)
    useful = useful & (reach <= 2)
    slot_of = jnp.where((apart > 0) == (side == 0), reach, reach + 2)
    slot_of = jnp.where(apart == 0, 0, slot_of)
    part_at = (candidate // part_blocks) % 2 != core
    place = (2 * slot_of + part_at.astype(jnp.int32)) * part_blocks + candidate % part_blocks
    earlier = jnp.arange(slots)[None, :] < jnp.arange(slots)[:, None]
    rank = jnp.sum((useful[:, None, :] & earlier[None]).astype(jnp.int32), axis=2)
    seat = useful[:, :, None] & (rank[:, :, None] == jnp.arange(slots)[None, None, :])

    def seated(values):
        return jnp.sum(jnp.where(seat, values[:, :, None], 0), axis=1).reshape(-1)

    query_positions = (
        block_ids[:, None] * BLOCK + jnp.arange(BLOCK, dtype=jnp.int32)[None, :]
    ).reshape(-1)
    query_first = token_docs(query_positions, doc_starts).reshape(half_blocks, BLOCK)
    query_end = token_ends(query_positions, doc_starts, total_blocks * BLOCK).reshape(
        half_blocks, BLOCK
    )
    lists = (
        seated(place),
        seated(candidate * BLOCK),
        seated(1 + nearby.astype(jnp.int32)),
        jnp.sum(useful.astype(jnp.int32), axis=1),
        jnp.concatenate([query_first, query_first], axis=1),
        jnp.concatenate([query_end, query_end], axis=1),
    )

    def project(rows, matrix, offset):
        return (jnp.dot(rows, matrix, preferred_element_type=f32) + offset).astype(bf16)

    rows_in = []
    for array in held:
        rows_in += [array, send(array, over_core)]
    query_rows = jnp.concatenate(
        [project(rows, query_matrix, query_offset) for rows in rows_in[:2]], axis=0
    ) * jnp.asarray(HEAD_DIM**-0.5, bf16)
    chunks = [project(rows, pair_matrix, pair_offset) for rows in rows_in]
    mixed = attend(lists, query_rows, chunks, groups, slots, few)
    mixed_given = send(mixed[local_rows:], over_core)
    mixed_kept = mixed[:local_rows]
    attended = pick(
        core,
        jnp.concatenate([mixed_kept, mixed_given], axis=1),
        jnp.concatenate([mixed_given, mixed_kept], axis=1),
    )

    first_sum = (
        inputs.astype(f32)
        + jnp.dot(attended, mixer_matrix, preferred_element_type=f32)
        + mixer_offset
    )
    middle, first_back = jax.vjp(norm_rows, first_sum, first_scale, first_level)
    middle_low = middle.astype(bf16)
    pre_act = jnp.dot(middle_low, expand_matrix, preferred_element_type=f32) + expand_offset
    active_wide, gelu_back = jax.vjp(gelu_exact, pre_act)
    active = active_wide.astype(bf16)
    second_sum = (
        middle + jnp.dot(active, shrink_matrix, preferred_element_type=f32) + shrink_offset
    )
    layer_out, second_back = jax.vjp(norm_rows, second_sum, second_scale, second_level)
    grad_second, second_scale_grad, second_level_grad = second_back(cotangent[0].astype(f32))
    grad_ffn = grad_second.astype(bf16)
    shrink_grad = jnp.einsum("tf,td->fd", active, grad_ffn, preferred_element_type=f32)
    shrink_bias_grad = jnp.sum(grad_ffn.astype(f32), axis=0)
    grad_active = jnp.einsum("td,fd->tf", grad_ffn, shrink_matrix, preferred_element_type=f32)
    grad_pre = gelu_back(grad_active)[0].astype(bf16)
    expand_grad = jnp.einsum("td,tf->df", middle_low, grad_pre, preferred_element_type=f32)
    expand_bias_grad = jnp.sum(grad_pre.astype(f32), axis=0)
    grad_middle = grad_second + jnp.einsum(
        "tf,df->td", grad_pre, expand_matrix, preferred_element_type=f32
    )
    grad_first, first_scale_grad, first_level_grad = first_back(grad_middle)
    grad_branch = grad_first.astype(bf16)
    mixer_grad = jnp.einsum("td,te->de", attended, grad_branch, preferred_element_type=f32)
    mixer_bias_grad = jnp.sum(grad_branch.astype(f32), axis=0)
    grad_attended = jnp.einsum(
        "te,de->td", grad_branch, mixer_matrix, preferred_element_type=f32
    ).astype(bf16)
    grad_kept = pick(core, grad_attended[:, :half_width], grad_attended[:, half_width:])
    grad_given = send(
        pick(core, grad_attended[:, half_width:], grad_attended[:, :half_width]), over_core
    )

    grad_bundle = jnp.concatenate(
        [
            expand_grad.astype(bf16).reshape(devices, wide_rows, model_width),
            shrink_grad.astype(bf16).reshape(devices, wide_rows, model_width),
            mixer_grad.astype(bf16).reshape(devices, own_rows, model_width),
        ],
        axis=1,
    ).reshape(-1, model_width)
    own_bundle = lax.psum_scatter(grad_bundle, axes, scatter_dimension=0, tiled=True).astype(f32)

    query_grad_rows, *pair_grads = attend_back(
        lists, query_rows, jnp.concatenate([grad_kept, grad_given], axis=0), chunks, groups, slots, few
    )
    query_grads = [query_grad_rows[:local_rows], query_grad_rows[local_rows:]]

    def back(grad, matrix):
        return jnp.einsum("te,de->td", grad, matrix, preferred_element_type=f32)

    partial = [back(grad, pair_matrix) for grad in pair_grads]
    partial[0] = partial[0] + back(query_grads[0], query_matrix)
    partial[1] = partial[1] + back(query_grads[1], query_matrix)
    totals = []
    for n in range(len(held)):
        totals.append(partial[2 * n] + send(partial[2 * n + 1].astype(bf16), over_core).astype(f32))
    own_total, beside_total, near_total, passed_total, far_total = totals
    near_total = near_total + send(passed_total.astype(bf16), over_side).astype(f32)
    input_grad = (
        grad_first
        + own_total
        + send(beside_total.astype(bf16), over_side).astype(f32)
        + send_back(far_total.astype(bf16), outward).astype(f32)
        + send_back(near_total.astype(bf16), inward).astype(f32)
    )

    pair_weight_grad = sum(
        jnp.einsum("td,te->de", rows, grad, preferred_element_type=f32)
        for rows, grad in zip(rows_in, pair_grads)
    )
    query_weight_grad = sum(
        jnp.einsum("td,te->de", rows, grad, preferred_element_type=f32)
        for rows, grad in zip(rows_in, query_grads)
    )
    value_bias_grad = sum(jnp.sum(grad[:, half_width:].astype(f32), axis=0) for grad in pair_grads)
    query_bias_grad = sum(jnp.sum(grad.astype(f32), axis=0) for grad in query_grads)

    def placed(half_row):
        nothing = jnp.zeros_like(half_row)
        return pick(
            core,
            jnp.concatenate([half_row, nothing]),
            jnp.concatenate([nothing, half_row]),
        )

    line_rows = jnp.stack(
        [
            placed(query_bias_grad),
            placed(value_bias_grad),
            mixer_bias_grad,
            first_scale_grad,
            first_level_grad,
            shrink_bias_grad,
            second_scale_grad,
            second_level_grad,
        ]
    )
    line_grads = jnp.concatenate([line_rows.T, expand_bias_grad.reshape(model_width, fold)], axis=1)
    stage = (2, 2, cycle_size * own_rows)
    table_grad = jnp.concatenate([pair_weight_grad, query_weight_grad], axis=1).reshape(
        stage + (trio,)
    )
    line_grads = line_grads.reshape(stage + (line_count,))
    kept = pick(core, table_grad[:, 0], table_grad[:, 1])
    kept_lines = pick(core, line_grads[:, 0], line_grads[:, 1])
    leaving = jnp.concatenate(
        [
            pick(core, table_grad[:, 1], table_grad[:, 0]).astype(bf16),
            split_low(pick(core, line_grads[:, 1], line_grads[:, 0]), line_width),
        ],
        axis=2,
    )
    arrived = send(leaving, over_core)
    brought = arrived[..., :trio].astype(f32)
    table_sum = pick(
        core,
        jnp.concatenate([kept, brought], axis=2),
        jnp.concatenate([brought, kept], axis=2),
    )
    line_sum = kept_lines + join_low(arrived[..., trio:], line_count)
    leaving = jnp.concatenate(
        [
            pick(side, table_sum[1], table_sum[0]).astype(bf16),
            split_low(pick(side, line_sum[1], line_sum[0]), line_width),
        ],
        axis=1,
    )
    arrived = send(leaving, over_side)
    table_sum = pick(side, table_sum[0], table_sum[1]) + arrived[:, : 2 * trio].astype(f32)
    line_sum = pick(side, line_sum[0], line_sum[1]) + join_low(arrived[:, 2 * trio :], line_count)
    leaving = jnp.concatenate([table_sum.astype(bf16), split_low(line_sum, line_width)], axis=1)
    arrived = lax.all_to_all(
        leaving.reshape(cycle_size, own_rows, -1), "blk", split_axis=0, concat_axis=0, tiled=True
    )
    table_own = jnp.sum(arrived[..., : 2 * trio].astype(f32), axis=0)
    line_own = jnp.sum(join_low(arrived[..., 2 * trio :], line_count), axis=0)

    def columns_of(which):
        low = which * half_width
        return jnp.concatenate(
            [table_own[:, low : low + half_width], table_own[:, trio + low : trio + low + half_width]],
            axis=1,
        )

    return (
        layer_out.astype(bf16)[None],
        input_grad[None],
        columns_of(2),
        line_own[:, 0],
        columns_of(0),
        columns_of(1),
        line_own[:, 1],
        own_bundle[2 * wide_rows :],
        line_own[:, 2],
        line_own[:, 3],
        line_own[:, 4],
        own_bundle[:wide_rows].reshape(own_rows, hidden),
        line_own[:, len(vectors) :].reshape(-1),
        own_bundle[wide_rows : 2 * wide_rows],
        line_own[:, 5],
        line_own[:, 6],
        line_own[:, 7],
    )


def solution(mesh):
    in_specs = (
        P("blk", "head", None),
        P(("head", "blk"), None),
        P(("head", "blk")),
        P(("head", "blk"), None),
        P(("head", "blk"), None),
        P(("head", "blk")),
        P(("head", "blk"), None),
        P(("head", "blk")),
        P(("head", "blk")),
        P(("head", "blk")),
        P(("head", "blk"), None),
        P(("head", "blk")),
        P(("head", "blk"), None),
        P(("head", "blk")),
        P(("head", "blk")),
        P(("head", "blk")),
        P(),
        P("blk", None),
        P("blk", "head", None),
    )
    out_specs = (
        P("blk", "head", None),
        P("blk", "head", None),
        P(("head", "blk"), None),
        P(("head", "blk")),
        P(("head", "blk"), None),
        P(("head", "blk"), None),
        P(("head", "blk")),
        P(("head", "blk"), None),
        P(("head", "blk")),
        P(("head", "blk")),
        P(("head", "blk")),
        P(("head", "blk"), None),
        P(("head", "blk")),
        P(("head", "blk"), None),
        P(("head", "blk")),
        P(("head", "blk")),
        P(("head", "blk")),
    )
    return jax.shard_map(body, mesh=mesh, in_specs=in_specs, out_specs=out_specs, check_vma=False)
```

time: 3900 us -> 718 us (0.18)
  local copies, waits for them, and re-layouts: 1660 us -> 83.8 us
  waiting for transfers between devices: 1000 us -> 197 us
  other arithmetic: 489 us -> 63.2 us
  matrix products: 575 us -> 213 us
  Pallas kernels: 0 us -> 99.3 us
  blocking collectives: 83.6 us -> 0 us
    reshape x76 -> x15, local copies, waits for them, and re-layouts: 543 us -> 24.7 us  [the longest x1 8.9 us: body(): expand_grad.astype(bf16).reshape(devices, wide_rows, model_width)]
    slice x48 -> x12, local copies, waits for them, and re-layouts: 323 us -> 17.6 us  [the longest x1 8.47 us: body(): bundles[:, wide_rows:2 * wide_rows].reshape(hidden, model_width)]
    dot_general x57 -> x36, matrix products: 408 us -> 112 us  [the longest x12 39.6 us: back(): return jnp.einsum('te,de->td', grad, matrix, preferred_element_type=f32)]
    reduce_scatter x3 -> x1, waiting for transfers between devices: 283 us -> 0.01 us  [body(): lax.psum_scatter(grad_bundle, axes, scatter_dimension=0, tiled=True)]
    gather x64 -> x0, local copies, waits for them, and re-layouts: 280 us -> none  [the longest x32 270 us: group_scores(): fetched = pool_now[group_local]]
    unnamed x15 -> x2, waiting for transfers between devices: 227 us -> 0.03 us
    scatter-add x8 -> x0, other arithmetic: 190 us -> none  [backward_group(): pool_grad = pool_grad.at[group_piece[4].reshape(-1)].add(update)]
    concatenate x9, local copies, waits for them, and re-layouts: 143 us -> 16.5 us  [the longest x1 5.2 us: body(): jnp.concatenate([pair_weight_grad, query_weight_grad], axis=1)]
  transfers between devices with their start and end apart: 20 -> 28, of which waited for: 15 -> 7; matrix products, arithmetic and copies ran while one was open for 24% -> 31% of each run, Pallas kernels for 0% -> 14%
where the time goes in v1:
time: 718 us; the launch traced here: 709 us
  matrix products  213 us (30%)
  waiting for transfers between devices  197 us (27%)
  Pallas kernels  99.3 us (14%)
  local copies, waits for them, and re-layouts  83.8 us (12%)
  other arithmetic  63.2 us (9%)
  starting transfers between devices  37.4 us (5%)
  between operations  15.6 us (2%)
    ppermute x22, waiting for transfers between devices, send(): return lax.ppermute(array, axes, pairs)  96.8 us
    all_to_all x1, waiting for transfers between devices, body(): lax.all_to_all(spread, 'blk', split_axis=0, concat_axis=0, tiled=True)  73.5 us
    pallas_call x1, Pallas kernels, attend_back(): pl.pallas_call(functools.partial(attend_back_kernel, (blocks, slots, few,...  61 us
    dot_general x12, matrix products, back(): return jnp.einsum('te,de->td', grad, matrix, preferred_element_type=f32)  39.6 us
    pallas_call x1, Pallas kernels, attend(): pl.pallas_call(functools.partial(attend_kernel, (blocks, slots, few, grou...  38.3 us
    dot_general x12, matrix products, project(): jnp.dot(rows, matrix, preferred_element_type=f32) + offset  36.8 us
    dot_general x1, matrix products, body(): jnp.dot(middle_low, expand_matrix, preferred_element_type=f32)  36.8 us
    dot_general x12, matrix products, body(): jnp.einsum('td,te->de', rows, grad, preferred_element_type=f32)  36 us
  transfers between devices with their start and end apart: 28, of which 7 were waited for; matrix products, arithmetic and copies ran while one was open for 31% of the time, Pallas kernels for 14%

profile of v1, /device:TPU:0, one launch (start us, length us, event | category | flops | bytes accessed | tf_op | source)
XLA Modules:
  0.0 709.5 jit_solution(12495744037192990772)
XLA Ops:
  14.7 5.9 collective-permute-start.3
  20.6 3.5 collective-permute-start.9
  26.3 3.7 all-to-all-start
  30.7 73.5 %all-to-all-done = bf16[8,24,2432]{2,1,0:T(8,128)(2,1)S(1)} async-done(((bf16[8,24,2432]{2,1,0:T(8,128)(2,1)}), bf16[8,24,2432]{2,1,0:T(8,128)(2,1)S(1)}, u32[]{:S(2)}, u32[]{:S(2)}) %all-to-all-start) | async-done | bytes 933920 | tf_op jit(solution)/shard_map/all_to_all | solution.py:444
  106.9 38.4 %collective-permute-done = bf16[192,2432]{1,0:T(8,128)(2,1)S(1)} collective-permute-done((bf16[192,2432]{1,0:T(8,128)(2,1)S(1)}, bf16[192,2432]{1,0:T(8,128)(2,1)S(1)}, u32[]{:S(2)}, u32[]{:S(2)}) %collective-permute-start) | collective-permute-done | bytes 933920 | tf_op jit(solution)/shard_map/ppermute | solution.py:401
  155.6 24.0 %collective-permute-done.7 = bf16[1024,768]{0,1:T(8,128)(2,1)} collective-permute-done((bf16[1024,768]{0,1:T(8,128)(2,1)}, bf16[1024,768]{0,1:T(8,128)(2,1)}, u32[]{:S(2)}, u32[]{:S(2)}) %collective-permute-start.7) | collective-permute-done | bytes 1572896 | tf_op jit(solution)/shard_map/ppermute | solution.py:401
  190.1 4.0 fusion.30.refs_13_.refs_14_
  194.1 4.0 fusion.25.refs_8_.refs_9_
  198.2 4.0 fusion.26.refs_9_.refs_10_
  202.2 4.0 fusion.28.refs_11_.refs_12_
  206.2 4.0 fusion.32.refs_15_.refs_16_
  210.1 2.8 fusion.27.refs_10_.refs_11_
  213.0 2.6 fusion.29.refs_12_.refs_13_
  215.6 2.6 fusion.33.refs_16_.refs_17_
  218.3 2.7 fusion.31.refs_14_.refs_15_
  221.0 38.3 %attend.1 = bf16[2048,384]{1,0:T(8,128)(2,1)} custom-call(s32[384]{0:T(512)} %reshape.1114.refs_0_, s32[384]{0:T(512)} %reshape.1115.refs_1_, s32[384]{0:T(512)} %reshape.1116.refs_2_, s32[32]{0:T(128)} %get-tuple-element.186.refs_3_, s32[32,128]{1,0:T(8,128)} %get-tuple-element.256.refs_4_, s32[32,128]{1,0:T(8,128)} %get-tuple-element.257.refs_5_, ...), custom_call_target="tpu_custom_call" | custom-call | flops 7247757312 | bytes 15728640 | tf_op jit(solution)/shard_map/attend/pallas_call | solution.py:228
  264.8 8.5 %fusion.136 = (bf16[32,96,768]{2,1,0:T(8,128)(2,1)}, bf16[32,96,768]{2,1,0:T(8,128)(2,1)}) fusion(bf16[32,216,768]{2,1,0:T(8,128)(2,1)} %bitcast.250), kind=kLoop, calls=%fused_computation.346 | loop fusion | bytes 18874368 | tf_op jit(solution)/shard_map/slice | solution.py:481
  273.3 3.5 fusion.143
  278.1 8.9 %reshape.1124 = bf16[768,3072]{1,0:T(8,128)(2,1)} reshape(bf16[32,96,768]{2,1,0:T(8,128)(2,1)} %get-tuple-element.193) | data formatting | bytes 9437184 | tf_op jit(solution)/shard_map/reshape | solution.py:480
  287.0 36.8 %multiply_convert_fusion = (bf16[1024,3072]{1,0:T(8,128)(2,1)S(1)}, f32[1024,3072]{1,0:T(8,128)}, f32[1024,3072]{1,0:T(8,128)}) fusion(f32[3072]{0:T(1024)S(1)} %reshape.1138, bf16[768,3072]{1,0:T(8,128)(2,1)} %reshape.1124, f32[1024,768]{0,1:T(8,128)S(1)} %get-tuple-element.244, f32[768]{0:T(1024)S(1)} %get-tuple-element.152, ...), kind=kOutput, calls=%fused_computation.4 | convolution fusion | flops 5043388416 | bytes 39348224 | tf_op jit(solution)/shard_map/dot_general | solution.py:552
  323.8 10.5 %fusion.144 = (f32[1024]{0:T(1024)S(1)}, f32[1024,768]{0,1:T(8,128)S(1)}) fusion(f32[768]{0:T(1024)S(1)} %get-tuple-element.151, bf16[1024,3072]{1,0:T(8,128)(2,1)S(1)} %get-tuple-element.184, bf16[3072,768]{1,0:T(8,128)(2,1)} %bitcast.277, f32[768]{0:T(1024)S(1)} %get-tuple-element.152, f32[768]{0:T(1024)S(1)} %get-tuple-element.153, ...), kind=kOutput, calls=%fused_computation.354 | convolution fusion | flops 4837342208 | bytes 17323008 | tf_op jit(solution)/shard_map/dot_general | solution.py:556
  336.8 2.8 convert_reduce_fusion.2
  339.6 17.0 %convert_reduce_fusion = (f32[3072]{0:T(1024)S(1)}, bf16[1024,3072]{1,0:T(8,128)(2,1)}) fusion(f32[1024,3072]{1,0:T(8,128)} %get-tuple-element.185, bf16[1024,768]{0,1:T(8,128)(2,1)S(1)} %get-tuple-element.179, bf16[3072,768]{1,0:T(8,128)(2,1)} %bitcast.278, f32[1024,3072]{1,0:T(8,128)} %get-tuple-element.245, f32[3072]{0:T(1024)S(1)} %reshape.1138), kind=kOutput, calls=%fused_computation.2 | convolution fusion | flops 4885312512 | bytes 37773312 | tf_op jit(solution)/shard_map/td,fd->tf/dot_general | solution.py:563
  356.6 10.7 %convolution_convert_fusion.1 = bf16[768,3072]{1,0:T(8,128)(2,1)} fusion(bf16[1024,3072]{1,0:T(8,128)(2,1)} %get-tuple-element.250, f32[1024,768]{0,1:T(8,128)} %copy-done.5, f32[768]{0:T(1024)S(1)} %get-tuple-element.152, f32[768]{0:T(1024)S(1)} %get-tuple-element.153, f32[1024]{0:T(1024)S(1)} %fusion.92, f32[1024]{0:T(1024)S(1)} %broadcast_multiply_fusion.2), kind=kOutput, calls=%fused_computation.20 | convolution fusion | flops 4838129664 | bytes 14170112 | tf_op jit(solution)/shard_map/td,tf->df/dot_general | solution.py:565
  367.3 9.9 %multiply_reduce_fusion = (f32[768]{0:T(1024)S(1)}, f32[1024]{0:T(1024)S(1)}, f32[768]{0:T(1024)S(1)}, f32[1024,768]{0,1:T(8,128)}) fusion(f32[1024,768]{0,1:T(8,128)S(1)} %copy-done.6, f32[1024]{0:T(1024)S(1)} %fusion.92, f32[1024]{0:T(1024)S(1)} %broadcast_multiply_fusion.2, f32[768]{0:T(1024)S(1)} %get-tuple-element.153, ...), kind=kOutput, calls=%fused_computation.34 | convolution fusion | flops 4845204480 | bytes 22061056 | tf_op jit(solution)/shard_map/tf,df->td/dot_general | solution.py:567
  377.2 6.9 convolution_convert_fusion
  384.1 8.9 %reshape.1132 = bf16[32,96,768]{2,1,0:T(8,128)(2,1)} reshape(bf16[768,3072]{1,0:T(8,128)(2,1)} %convolution_convert_fusion.1) | data formatting | bytes 9437184 | tf_op jit(solution)/shard_map/reshape | solution.py:584
  393.0 3.7 fusion.131
  401.2 3.6 convolution_convert_fusion.7
  404.9 5.0 pad_maximum_fusion
  413.2 2.6 copy.331
  415.8 2.8 pad_maximum_fusion.2.refs_7_
  418.6 61.0 %attend_back.1 = (bf16[2048,384]{1,0:T(8,128)(2,1)}, bf16[1024,768]{1,0:T(8,128)(2,1)}, bf16[1024,768]{1,0:T(8,128)(2,1)}, bf16[1024,768]{1,0:T(8,128)(2,1)}, bf...) custom-call(s32[384]{0:T(512)} %reshape.1114.refs_0_, ...), custom_call_target="tpu_custom_call" | custom-call | flops 18119393280 | bytes 31457280 | tf_op jit(solution)/shard_map/attend_back/pallas_call | solution.py:256
  480.9 4.9 fusion.17
  494.9 2.6 fusion.49
  503.1 3.1 fusion.150
  507.7 3.2 fusion.145
  510.9 3.0 fusion.146
  513.9 4.4 fusion.148
  518.2 4.4 fusion.151
  522.7 4.3 add_bitcast_fusion.1
  527.0 3.3 pad_maximum_fusion.1
  530.3 5.2 copy.328
  539.7 3.1 fusion.47
  543.4 3.5 concatenate.137
  549.6 2.6 convolution_convert_fusion.5
  554.7 2.6 convolution_convert_fusion.2
  557.9 2.6 convolution_convert_fusion.4
  568.3 4.6 convolution_convert_fusion.3
  573.4 3.1 fusion.110
  577.0 4.2 add_convert_fusion.2
  581.2 9.0 %collective-permute-done.23 = bf16[192,2432]{1,0:T(8,128)(2,1)S(1)} collective-permute-done((bf16[192,2432]{1,0:T(8,128)(2,1)}, bf16[192,2432]{1,0:T(8,128)(2,1)S(1)}, u32[]{:S(2)}, u32[]{:S(2)}) %collective-permute-start.23) | collective-permute-done | bytes 933920 | tf_op jit(solution)/shard_map/ppermute | solution.py:401
  594.5 7.3 %all-to-all-start.1 = ((bf16[8,24,2432]{2,1,0:T(8,128)(2,1)}), bf16[8,24,2432]{2,1,0:T(8,128)(2,1)}, u32[]{:S(2)}, u32[]{:S(2)}) async-start(bf16[8,24,2432]{2,1,0:T(8,128)(2,1)} %bitcast.282), calls=%async_computation.1 | async-start | bytes 1867776 | tf_op jit(solution)/shard_map/all_to_all | solution.py:681
  601.8 5.0 add_convert_fusion.4
  607.1 4.1 add_convert_fusion.3
  612.8 15.0 %collective-permute-done.20 = bf16[1024,768]{0,1:T(8,128)(2,1)} collective-permute-done((bf16[1024,768]{0,1:T(8,128)(2,1)}, bf16[1024,768]{0,1:T(8,128)(2,1)}, u32[]{:S(2)}, u32[]{:S(2)}) %collective-permute-start.20) | collective-permute-done | bytes 1572896 | tf_op jit(solution)/shard_map/ppermute | solution.py:401
  627.9 3.9 add_convert_fusion.1
  631.8 6.2 collective-permute-start.21
  638.0 2.8 fusion.54
  640.7 3.1 fusion.117
  649.5 10.2 %collective-permute-done.15 = bf16[1024,768]{0,1:T(8,128)(2,1)} collective-permute-done((bf16[1024,768]{0,1:T(8,128)(2,1)}, bf16[1024,768]{0,1:T(8,128)(2,1)}, u32[]{:S(2)}, u32[]{:S(2)}) %collective-permute-start.15) | collective-permute-done | bytes 1572896 | tf_op jit(solution)/shard_map/ppermute | solution.py:401
  659.7 27.0 %collective-permute-done.21 = bf16[1024,768]{0,1:T(8,128)(2,1)} collective-permute-done((bf16[1024,768]{0,1:T(8,128)(2,1)}, bf16[1024,768]{0,1:T(8,128)(2,1)}, u32[]{:S(2)}, u32[]{:S(2)}) %collective-permute-start.21) | collective-permute-done | bytes 1572896 | tf_op jit(solution)/shard_map/ppermute | solution.py:404
  686.7 8.2 %add_bitcast_fusion = f32[1,1024,768]{1,2,0:T(8,128)} fusion(bf16[1024,768]{0,1:T(8,128)(2,1)} %collective-permute-done.21, bf16[1024,768]{0,1:T(8,128)(2,1)} %collective-permute-done.17, bf16[1024,768]{0,1:T(8,128)(2,1)} %collective-permute-done.15, bf16[1024,768]{0,1:T(8,128)(2,1)} %collective-permute-done.13, f32[1024,768]{0,1:T(8,128)} %fusion.117, ...), kind=kLoop, calls=%fused_computation.36 | loop fusion | flops 8650752 | bytes 18878464 | tf_op jit(solution)/shard_map/broadcast_in_dim | solution.py:696
  695.0 3.5 copy.332
  (401 shorter events, 102.7 us)
Async XLA Ops:
  7.2 256.2 %all-gather.2.cloned.1.call-start = ((), (), s32[]{:S(2)}) async-start(), calls=%async_computation.3 | async-start | bytes 10948608 | tf_op jit(solution)/shard_map/all_gather | solution.py:477
  8.4 15.7 %copy-start.55 = (f32[24,768]{1,0:T(8,128)S(1)}, f32[24,768]{1,0:T(8,128)}, u32[]{:S(2)}) copy-start(f32[24,768]{1,0:T(8,128)} %param.23) | copy-start | bytes 221188
  8.5 15.7 %copy-start.56 = (f32[24,768]{1,0:T(8,128)S(1)}, f32[24,768]{1,0:T(8,128)}, u32[]{:S(2)}) copy-start(f32[24,768]{1,0:T(8,128)} %param.20) | copy-start | bytes 221188
  8.5 15.7 %copy-start.57 = (f32[24,768]{1,0:T(8,128)S(1)}, f32[24,768]{1,0:T(8,128)}, u32[]{:S(2)}) copy-start(f32[24,768]{1,0:T(8,128)} %param.22) | copy-start | bytes 221188
  9.5 14.7 %copy-start.74 = (f32[24]{0:T(128)S(1)}, f32[24]{0:T(128)}, u32[]{:S(2)}) copy-start(f32[24]{0:T(128)} %param.21) | copy-start | bytes 292
  9.5 14.8 %copy-start.75 = (f32[24]{0:T(128)S(1)}, f32[24]{0:T(128)}, u32[]{:S(2)}) copy-start(f32[24]{0:T(128)} %param.24) | copy-start | bytes 292
  9.5 14.9 %copy-start.76 = (f32[24]{0:T(128)S(1)}, f32[24]{0:T(128)}, u32[]{:S(2)}) copy-start(f32[24]{0:T(128)} %param.26) | copy-start | bytes 292
  9.5 15.0 %copy-start.77 = (f32[24]{0:T(128)S(1)}, f32[24]{0:T(128)}, u32[]{:S(2)}) copy-start(f32[24]{0:T(128)} %param.27) | copy-start | bytes 292
  9.5 15.1 %copy-start.78 = (f32[24]{0:T(128)S(1)}, f32[24]{0:T(128)}, u32[]{:S(2)}) copy-start(f32[24]{0:T(128)} %param.28) | copy-start | bytes 292
  9.6 15.2 %copy-start.79 = (f32[24]{0:T(128)S(1)}, f32[24]{0:T(128)}, u32[]{:S(2)}) copy-start(f32[24]{0:T(128)} %param.32) | copy-start | bytes 292
  9.6 15.3 %copy-start.80 = (f32[24]{0:T(128)S(1)}, f32[24]{0:T(128)}, u32[]{:S(2)}) copy-start(f32[24]{0:T(128)} %param.33) | copy-start | bytes 292
  9.6 15.4 %copy-start.81 = (f32[24]{0:T(128)S(1)}, f32[24]{0:T(128)}, u32[]{:S(2)}) copy-start(f32[24]{0:T(128)} %param.34) | copy-start | bytes 292
  9.6 15.5 %copy-start.82 = (f32[96]{0:T(128)S(1)}, f32[96]{0:T(128)}, u32[]{:S(2)}) copy-start(f32[96]{0:T(128)} %param.30) | copy-start | bytes 1156
  13.0 17.2 %copy-start.63 = (s32[64,3]{0,1:T(4,128)S(1)}, s32[64,3]{0,1:T(4,128)}, u32[]{:S(2)}) copy-start(s32[64,3]{0,1:T(4,128)} %param.36) | copy-start | bytes 2308
  13.0 17.3 %copy-start.66 = (s32[12]{0:T(128)S(1)}, s32[12]{0:T(128)}, u32[]{:S(2)}) copy-start(s32[12]{0:T(128)} %param.35) | copy-start | bytes 148
  13.0 170.7 %collective-permute-start.2 = (bf16[1024,768]{0,1:T(8,128)(2,1)}, bf16[1024,768]{0,1:T(8,128)(2,1)}, u32[]{:S(2)}, u32[]{:S(2)}) collective-permute-start(bf16[1024,768]{0,1:T(8,128)(2,1)} %bitcast), channel_id=1, source_target_pairs={{0,8},{1,9},{2,10},{3,11},{4,12},{5,13},{6,14},{7,15},{8,0},{9,1},... | collective-permute-start | bytes 4718600 | tf_op jit(solution)/shard_map/ppermute | solution.py:401
  13.4 92.1 %collective-permute-start.5 = (bf16[1024,768]{0,1:T(8,128)(2,1)}, bf16[1024,768]{0,1:T(8,128)(2,1)}, u32[]{:S(2)}, u32[]{:S(2)}) collective-permute-start(bf16[1024,768]{0,1:T(8,128)(2,1)} %bitcast), channel_id=1, source_target_pairs={{1,0},{2,1},{3,2},{4,3},{5,4},{6,5},{7,6},{9,8},{10,9},{11,10},{12... | collective-permute-start | bytes 4718600 | tf_op jit(solution)/shard_map/ppermute | solution.py:401
  14.7 140.3 %collective-permute-start.3 = (bf16[1024,768]{0,1:T(8,128)(2,1)}, bf16[1024,768]{0,1:T(8,128)(2,1)}, u32[]{:S(2)}, u32[]{:S(2)}) collective-permute-start(bf16[1024,768]{0,1:T(8,128)(2,1)} %bitcast), channel_id=1, source_target_pairs={{0,16},{1,17},{2,18},{3,19},{4,20},{5,21},{6,22},{7,23},{8,24},{9,... | collective-permute-start | bytes 4718600 | tf_op jit(solution)/shard_map/ppermute | solution.py:401
  20.6 134.9 %collective-permute-start.9 = (bf16[1024,768]{0,1:T(8,128)(2,1)}, bf16[1024,768]{0,1:T(8,128)(2,1)}, u32[]{:S(2)}, u32[]{:S(2)}) collective-permute-start(bf16[1024,768]{0,1:T(8,128)(2,1)} %bitcast), channel_id=1, source_target_pairs={{0,1},{1,2},{2,3},{3,4},{4,5},{5,6},{6,7},{8,9},{9,10},{10,11},{11... | collective-permute-start | bytes 4718600 | tf_op jit(solution)/shard_map/ppermute | solution.py:401
  26.3 77.9 %all-to-all-start = ((bf16[8,24,2432]{2,1,0:T(8,128)(2,1)}), bf16[8,24,2432]{2,1,0:T(8,128)(2,1)S(1)}, u32[]{:S(2)}, u32[]{:S(2)}) async-start(bf16[8,24,2432]{2,1,0:T(8,128)(2,1)} %broadcast_in_dim.201), calls=%async_computation | async-start | bytes 1867776 | tf_op jit(solution)/shard_map/all_to_all | solution.py:444
  30.0 668.5 %reduce-scatter.2.cloned.1.call-start = ((), (), s32[]{:S(2)}) async-start(), calls=%async_computation.4 | async-start | bytes 10948608 | tf_op jit(solution)/shard_map/reduce_scatter | solution.py:590
  30.1 74.1 %copy-start.64 = (s32[32]{0:T(128)}, s32[32]{0:T(128)S(1)}, u32[]{:S(2)}) copy-start(s32[32]{0:T(128)S(1)} %get-tuple-element.188) | copy-start | bytes 388
  104.2 41.2 %collective-permute-start = (bf16[192,2432]{1,0:T(8,128)(2,1)S(1)}, bf16[192,2432]{1,0:T(8,128)(2,1)S(1)}, u32[]{:S(2)}, u32[]{:S(2)}) collective-permute-start(bf16[192,2432]{1,0:T(8,128)(2,1)S(1)} %bitcast.283), channel_id=1, source_target_pairs={{0,16},{1,17},{2,18},{3,19},{4,20},{5,21},{6,22},{7,23},{8,24},{9,... | collective-permute-start | bytes 2801672 | tf_op jit(solution)/shard_map/ppermute | solution.py:401
  105.5 74.2 %collective-permute-start.7 = (bf16[1024,768]{0,1:T(8,128)(2,1)}, bf16[1024,768]{0,1:T(8,128)(2,1)}, u32[]{:S(2)}, u32[]{:S(2)}) collective-permute-start(bf16[1024,768]{0,1:T(8,128)(2,1)} %collective-permute-done.5), channel_id=1, source_target_pairs={{0,16},{1,17},{2,18},{3,19},{4,20},{5,21},{6,22},{7,23},{8,24},{9,... | collective-permute-start | bytes 4718600 | tf_op jit(solution)/shard_map/ppermute | solution.py:401
  147.0 32.7 %collective-permute-start.1 = (bf16[2,192,1280]{2,1,0:T(8,128)(2,1)}, bf16[2,192,1280]{2,1,0:T(8,128)(2,1)S(1)}, u32[]{:S(2)}, u32[]{:S(2)}) collective-permute-start(bf16[2,192,1280]{2,1,0:T(8,128)(2,1)} %get-tuple-element.212), channel_id=1, source_target_pairs={{0,8},{1,9},{2,10},{3,11},{4,12},{5,13},{6,14},{7,15},{8,0},{9,1},... | collective-permute-start | bytes 2949128 | tf_op jit(solution)/shard_map/ppermute | solution.py:401
  152.5 28.0 %copy-start = (bf16[1,1024,768]{1,2,0:T(8,128)(2,1)}, bf16[1,1024,768]{1,2,0:T(8,128)(2,1)S(1)}, u32[]{:S(2)}) copy-start(bf16[1,1024,768]{1,2,0:T(8,128)(2,1)S(1)} %copy.314) | copy-start | bytes 4718596
  155.0 58.0 %collective-permute-start.6 = (bf16[1024,768]{0,1:T(8,128)(2,1)}, bf16[1024,768]{0,1:T(8,128)(2,1)S(1)}, u32[]{:S(2)}, u32[]{:S(2)}) collective-permute-start(bf16[1024,768]{0,1:T(8,128)(2,1)} %collective-permute-done.5), channel_id=1, source_target_pairs={{0,8},{1,9},{2,10},{3,11},{4,12},{5,13},{6,14},{7,15},{8,0},{9,1},... | collective-permute-start | bytes 4718600 | tf_op jit(solution)/shard_map/ppermute | solution.py:401
  155.5 54.6 %collective-permute-start.4 = (bf16[1024,768]{0,1:T(8,128)(2,1)}, bf16[1024,768]{0,1:T(8,128)(2,1)S(1)}, u32[]{:S(2)}, u32[]{:S(2)}) collective-permute-start(bf16[1024,768]{0,1:T(8,128)(2,1)} %collective-permute-done.3), channel_id=1, source_target_pairs={{0,8},{1,9},{2,10},{3,11},{4,12},{5,13},{6,14},{7,15},{8,0},{9,1},... | collective-permute-start | bytes 4718600 | tf_op jit(solution)/shard_map/ppermute | solution.py:401
  179.6 36.0 %collective-permute-start.10 = (bf16[1024,768]{0,1:T(8,128)(2,1)}, bf16[1024,768]{0,1:T(8,128)(2,1)S(1)}, u32[]{:S(2)}, u32[]{:S(2)}) collective-permute-start(bf16[1024,768]{0,1:T(8,128)(2,1)} %collective-permute-done.9), channel_id=1, source_target_pairs={{0,8},{1,9},{2,10},{3,11},{4,12},{5,13},{6,14},{7,15},{8,0},{9,1},... | collective-permute-start | bytes 4718600 | tf_op jit(solution)/shard_map/ppermute | solution.py:401
  179.7 38.6 %collective-permute-start.8 = (bf16[1024,768]{0,1:T(8,128)(2,1)}, bf16[1024,768]{0,1:T(8,128)(2,1)S(1)}, u32[]{:S(2)}, u32[]{:S(2)}) collective-permute-start(bf16[1024,768]{0,1:T(8,128)(2,1)} %collective-permute-done.7), channel_id=1, source_target_pairs={{0,8},{1,9},{2,10},{3,11},{4,12},{5,13},{6,14},{7,15},{8,0},{9,1},... | collective-permute-start | bytes 4718600 | tf_op jit(solution)/shard_map/ppermute | solution.py:401
  180.6 81.1 %copy-start.7 = (bf16[2,2,192,1280]{3,2,1,0:T(8,128)(2,1)}, bf16[2,2,192,1280]{3,2,1,0:T(8,128)(2,1)S(1)}, u32[]{:S(2)}) copy-start(bf16[2,2,192,1280]{3,2,1,0:T(8,128)(2,1)S(1)} %copy.301) | copy-start | bytes 5898244
  261.7 11.5 %collective-permute-start.11 = (bf16[1024,384]{1,0:T(8,128)(2,1)S(1)}, bf16[1024,384]{1,0:T(8,128)(2,1)}, u32[]{:S(2)}, u32[]{:S(2)}) collective-permute-start(bf16[1024,384]{1,0:T(8,128)(2,1)S(1)} %get-tuple-element.200), channel_id=1, source_target_pairs={{0,8},{1,9},{2,10},{3,11},{4,12},{5,13},{6,14},{7,15},{8,0},{9,1},... | collective-permute-start | bytes 2359304 | tf_op jit(solution)/shard_map/ppermute | solution.py:401
  264.8 8.5 %copy-start.29 = (bf16[32,24,768]{2,1,0:T(8,128)(2,1)}, bf16[32,24,768]{2,1,0:T(8,128)(2,1)S(1)}, u32[]{:S(2)}) copy-start(bf16[32,24,768]{2,1,0:T(8,128)(2,1)S(1)} %slice.465) | copy-start | bytes 3538948
  264.8 8.5 %copy-start.31 = (bf16[1024,384]{1,0:T(8,128)(2,1)S(1)}, bf16[1024,384]{1,0:T(8,128)(2,1)}, u32[]{:S(2)}) copy-start(bf16[1024,384]{1,0:T(8,128)(2,1)} %get-tuple-element.199) | copy-start | bytes 2359300
  276.8 10.2 %copy-start.5 = (f32[1024,768]{0,1:T(8,128)}, f32[1024,768]{0,1:T(8,128)S(1)}, u32[]{:S(2)}) copy-start(f32[1024,768]{0,1:T(8,128)S(1)} %get-tuple-element.244) | copy-start | bytes 9437188
  323.8 10.6 %copy-start.84 = (bf16[1024,3072]{1,0:T(8,128)(2,1)}, bf16[1024,3072]{1,0:T(8,128)(2,1)S(1)}, u32[]{:S(2)}) copy-start(bf16[1024,3072]{1,0:T(8,128)(2,1)S(1)} %get-tuple-element.184) | copy-start | bytes 18874372
  323.8 10.6 %copy-start.1 = (bf16[1,1024,768]{1,2,0:T(8,128)(2,1)S(1)}, bf16[1,1024,768]{1,2,0:T(8,128)(2,1)}, u32[]{:S(2)}) copy-start(bf16[1,1024,768]{1,2,0:T(8,128)(2,1)} %copy-done) | copy-start | bytes 4718596
  356.6 10.7 %copy-start.6 = (f32[1024,768]{0,1:T(8,128)S(1)}, f32[1024,768]{0,1:T(8,128)}, u32[]{:S(2)}) copy-start(f32[1024,768]{0,1:T(8,128)} %copy-done.5) | copy-start | bytes 9437188
  356.6 10.7 %copy-start.83 = (bf16[1024,3072]{1,0:T(8,128)(2,1)S(1)}, bf16[1024,3072]{1,0:T(8,128)(2,1)}, u32[]{:S(2)}) copy-start(bf16[1024,3072]{1,0:T(8,128)(2,1)} %get-tuple-element.250) | copy-start | bytes 18874372
  356.6 20.6 %slice-start.4 = ((s8[6291456]{0:T(1024)(128)(4,1)}), s8[4194304]{0:T(1024)(128)(4,1)S(1)}, s32[]{:S(2)}) async-start(s8[6291456]{0:T(1024)(128)(4,1)} %bitcast.301), calls=%async_computation.9 | async-start | bytes 8388608
  367.3 9.9 %slice-start.5 = ((s8[6291456]{0:T(1024)(128)(4,1)}), s8[2097152]{0:T(1024)(128)(4,1)S(1)}, s32[]{:S(2)}) async-start(s8[6291456]{0:T(1024)(128)(4,1)} %bitcast.301), calls=%async_computation.10 | async-start | bytes 4194304
  384.1 8.9 %copy-start.59 = (f32[1024]{0:T(1024)S(1)}, f32[1024]{0:T(1024)}, u32[]{:S(2)}) copy-start(f32[1024]{0:T(1024)} %copy-done.58) | copy-start | bytes 12292
  400.7 15.1 %collective-permute-start.12 = (bf16[1024,384]{1,0:T(8,128)(2,1)}, bf16[1024,384]{1,0:T(8,128)(2,1)}, u32[]{:S(2)}, u32[]{:S(2)}) collective-permute-start(bf16[1024,384]{1,0:T(8,128)(2,1)} %get-tuple-element.198), channel_id=1, source_target_pairs={{0,8},{1,9},{2,10},{3,11},{4,12},{5,13},{6,14},{7,15},{8,0},{9,1},... | collective-permute-start | bytes 2359304 | tf_op jit(solution)/shard_map/ppermute | solution.py:401
  480.9 6.6 copy-start.37
  480.9 6.7 copy-start.50
  480.9 6.9 copy-start.47
  480.9 7.8 %copy-start.45 = (bf16[1024,768]{1,0:T(8,128)(2,1)S(1)}, bf16[1024,768]{1,0:T(8,128)(2,1)}, u32[]{:S(2)}) copy-start(bf16[1024,768]{1,0:T(8,128)(2,1)} %get-tuple-element.36) | copy-start | bytes 4718596
  547.0 13.7 %collective-permute-start.22 = (bf16[2,192,1280]{2,1,0:T(8,128)(2,1)}, bf16[2,192,1280]{2,1,0:T(8,128)(2,1)S(1)}, u32[]{:S(2)}, u32[]{:S(2)}) collective-permute-start(bf16[2,192,1280]{2,1,0:T(8,128)(2,1)} %concatenate.137), channel_id=1, source_target_pairs={{0,8},{1,9},{2,10},{3,11},{4,12},{5,13},{6,14},{7,15},{8,0},{9,1},... | collective-permute-start | bytes 2949128 | tf_op jit(solution)/shard_map/ppermute | solution.py:401
  557.3 19.2 %collective-permute-start.19 = (bf16[1024,768]{0,1:T(8,128)(2,1)}, bf16[1024,768]{0,1:T(8,128)(2,1)}, u32[]{:S(2)}, u32[]{:S(2)}) collective-permute-start(bf16[1024,768]{0,1:T(8,128)(2,1)} %convolution_convert_fusion.2), channel_id=1, source_target_pairs={{0,8},{1,9},{2,10},{3,11},{4,12},{5,13},{6,14},{7,15},{8,0},{9,1},... | collective-permute-start | bytes 4718600 | tf_op jit(solution)/shard_map/ppermute | solution.py:401
  567.4 22.8 %collective-permute-start.23 = (bf16[192,2432]{1,0:T(8,128)(2,1)}, bf16[192,2432]{1,0:T(8,128)(2,1)S(1)}, u32[]{:S(2)}, u32[]{:S(2)}) collective-permute-start(bf16[192,2432]{1,0:T(8,128)(2,1)} %concatenate.140), channel_id=1, source_target_pairs={{0,16},{1,17},{2,18},{3,19},{4,20},{5,21},{6,22},{7,23},{8,24},{9,... | collective-permute-start | bytes 2801672 | tf_op jit(solution)/shard_map/ppermute | solution.py:401
  572.9 76.6 %collective-permute-start.13 = (bf16[1024,768]{0,1:T(8,128)(2,1)}, bf16[1024,768]{0,1:T(8,128)(2,1)}, u32[]{:S(2)}, u32[]{:S(2)}) collective-permute-start(bf16[1024,768]{0,1:T(8,128)(2,1)} %add_convert_fusion.5), channel_id=1, source_target_pairs={{0,8},{1,9},{2,10},{3,11},{4,12},{5,13},{6,14},{7,15},{8,0},{9,1},... | collective-permute-start | bytes 4718600 | tf_op jit(solution)/shard_map/ppermute | solution.py:401
  572.9 28.9 %collective-permute-start.14 = (bf16[1024,768]{0,1:T(8,128)(2,1)}, bf16[1024,768]{0,1:T(8,128)(2,1)}, u32[]{:S(2)}, u32[]{:S(2)}) collective-permute-start(bf16[1024,768]{0,1:T(8,128)(2,1)} %convolution_convert_fusion.5), channel_id=1, source_target_pairs={{0,8},{1,9},{2,10},{3,11},{4,12},{5,13},{6,14},{7,15},{8,0},{9,1},... | collective-permute-start | bytes 4718600 | tf_op jit(solution)/shard_map/ppermute | solution.py:401
  573.4 33.7 %collective-permute-start.16 = (bf16[1024,768]{0,1:T(8,128)(2,1)}, bf16[1024,768]{0,1:T(8,128)(2,1)}, u32[]{:S(2)}, u32[]{:S(2)}) collective-permute-start(bf16[1024,768]{0,1:T(8,128)(2,1)} %convolution_convert_fusion.4), channel_id=1, source_target_pairs={{0,8},{1,9},{2,10},{3,11},{4,12},{5,13},{6,14},{7,15},{8,0},{9,1},... | collective-permute-start | bytes 4718600 | tf_op jit(solution)/shard_map/ppermute | solution.py:401
  576.5 14.6 %copy-start.21 = (f32[2,192,12]{2,1,0:T(8,128)S(1)}, f32[2,192,12]{2,1,0:T(8,128)}, u32[]{:S(2)}) copy-start(f32[2,192,12]{2,1,0:T(8,128)} %copy-done.20) | copy-start | bytes 55300
  576.5 36.3 %collective-permute-start.18 = (bf16[1024,768]{0,1:T(8,128)(2,1)}, bf16[1024,768]{0,1:T(8,128)(2,1)}, u32[]{:S(2)}, u32[]{:S(2)}) collective-permute-start(bf16[1024,768]{0,1:T(8,128)(2,1)} %convolution_convert_fusion.3), channel_id=1, source_target_pairs={{0,8},{1,9},{2,10},{3,11},{4,12},{5,13},{6,14},{7,15},{8,0},{9,1},... | collective-permute-start | bytes 4718600 | tf_op jit(solution)/shard_map/ppermute | solution.py:401
  577.0 14.2 %copy-start.3 = (f32[2,192,2304]{2,1,0:T(8,128)S(1)}, f32[2,192,2304]{2,1,0:T(8,128)}, u32[]{:S(2)}) copy-start(f32[2,192,2304]{2,1,0:T(8,128)} %copy-done.2) | copy-start | bytes 10616836
  590.2 37.6 %collective-permute-start.20 = (bf16[1024,768]{0,1:T(8,128)(2,1)}, bf16[1024,768]{0,1:T(8,128)(2,1)}, u32[]{:S(2)}, u32[]{:S(2)}) collective-permute-start(bf16[1024,768]{0,1:T(8,128)(2,1)} %add_convert_fusion.2), channel_id=1, source_target_pairs={{0,16},{1,17},{2,18},{3,19},{4,20},{5,21},{6,22},{7,23},{8,24},{9,... | collective-permute-start | bytes 4718600 | tf_op jit(solution)/shard_map/ppermute | solution.py:401
  594.5 49.4 %all-to-all-start.1 = ((bf16[8,24,2432]{2,1,0:T(8,128)(2,1)}), bf16[8,24,2432]{2,1,0:T(8,128)(2,1)}, u32[]{:S(2)}, u32[]{:S(2)}) async-start(bf16[8,24,2432]{2,1,0:T(8,128)(2,1)} %bitcast.282), calls=%async_computation.1 | async-start | bytes 1867776 | tf_op jit(solution)/shard_map/all_to_all | solution.py:681
  606.8 21.1 %copy-start.18 = (f32[1024,768]{0,1:T(8,128)S(1)}, f32[1024,768]{0,1:T(8,128)}, u32[]{:S(2)}) copy-start(f32[1024,768]{0,1:T(8,128)} %fusion.110) | copy-start | bytes 9437188
  606.8 52.9 %collective-permute-start.15 = (bf16[1024,768]{0,1:T(8,128)(2,1)}, bf16[1024,768]{0,1:T(8,128)(2,1)}, u32[]{:S(2)}, u32[]{:S(2)}) collective-permute-start(bf16[1024,768]{0,1:T(8,128)(2,1)} %add_convert_fusion.4), channel_id=1, source_target_pairs={{0,16},{1,17},{2,18},{3,19},{4,20},{5,21},{6,22},{7,23},{8,24},{9,... | collective-permute-start | bytes 4718600 | tf_op jit(solution)/shard_map/ppermute | solution.py:401
  611.2 26.7 %copy-start.14 = (bf16[2048,384]{1,0:T(8,128)(2,1)S(1)}, bf16[2048,384]{1,0:T(8,128)(2,1)}, u32[]{:S(2)}) copy-start(bf16[2048,384]{1,0:T(8,128)(2,1)} %get-tuple-element.29) | copy-start | bytes 4718596
  611.2 48.5 %collective-permute-start.17 = (bf16[1024,768]{0,1:T(8,128)(2,1)}, bf16[1024,768]{0,1:T(8,128)(2,1)}, u32[]{:S(2)}, u32[]{:S(2)}) collective-permute-start(bf16[1024,768]{0,1:T(8,128)(2,1)} %add_convert_fusion.3), channel_id=1, source_target_pairs={{1,0},{2,1},{3,2},{4,3},{5,4},{6,5},{7,6},{9,8},{10,9},{11,10},{12... | collective-permute-start | bytes 4718600 | tf_op jit(solution)/shard_map/ppermute | solution.py:404
  631.8 9.0 %copy-start.33 = (bf16[1024,768]{1,0:T(8,128)(2,1)S(1)}, bf16[1024,768]{1,0:T(8,128)(2,1)}, u32[]{:S(2)}) copy-start(bf16[1024,768]{1,0:T(8,128)(2,1)} %get-tuple-element.28) | copy-start | bytes 4718596
  631.8 55.0 %collective-permute-start.21 = (bf16[1024,768]{0,1:T(8,128)(2,1)}, bf16[1024,768]{0,1:T(8,128)(2,1)}, u32[]{:S(2)}, u32[]{:S(2)}) collective-permute-start(bf16[1024,768]{0,1:T(8,128)(2,1)} %add_convert_fusion.1), channel_id=1, source_target_pairs={{0,1},{1,2},{2,3},{3,4},{4,5},{5,6},{6,7},{8,9},{9,10},{10,11},{11... | collective-permute-start | bytes 4718600 | tf_op jit(solution)/shard_map/ppermute | solution.py:404
  (55 other events, 164.0 us)
Sparse Core Ops, SparseCore 0:
  11.4 152.4 all-gather.1
  410.0 143.4 reduce-scatter.1
